TPU v7x, 256 devices: a whole 4x4x8 slice. The times are simulated.
256 devices in a mesh: group: 16 (over z, x_lo), section: 2 (over x_hi), tensor: 8 (over y, core).
Axes of the slice: x: 4 (x_hi: 2, x_lo: 2; x = x_hi * 2 + x_lo), y: 4, z: 8, core: 2. Of those that a mesh axis runs over, the one named last changes fastest.
Arguments:
- prompt_tokens: bfloat16 [512, 128, 8192], P(('group', 'section'), None, 'tensor'), may hold values from -6 to 6
- kv_weight: bfloat16 [8192, 2048], P('tensor'), may hold values from -0.0625 to 0.0625
- routes: int32 [512, 1], replicated, may hold values from 0 to 15; in each aligned block of 16 rows (0 to 15, 16 to 31, ...) at most 2 rows name the same one
- lengths: int32 [512], replicated, may hold values from 1 to 128, 40960 in all
- queries: bfloat16 [16, 2, 16, 2, 4, 8192], P('group', 'section', None, None, None, 'tensor'), may hold values from -6 to 6
- new_kv: bfloat16 [16, 2, 16, 2, 4, 2048], P('group', 'section', None, None, None, 'tensor'), may hold values from -6 to 6
Outputs:
- decode_cache: bfloat16 [16, 2, 16, 2, 2048, 128], P('group', 'section', None, None, 'tensor')
- attention: bfloat16 [16, 2, 16, 2, 4, 8192], P('group', 'section', None, None, None, 'tensor')
Inputs may be any that keep to these rules, and one draw needn't show every extreme that they name: `routes`: in each block of 16 prompts (those of one group and section index) no decode group is named more than 2 times, and some block names one group exactly 2 times.
All inputs are finite; a program needn't handle non-finite values.
Results may differ from a plain program's by a relative error of at most 0.017.
Values may be sent and summed in bfloat16 or wider, within the bound.
No kernel may reach another device: no remote copies, remote signals or barrier semaphores. Data moves between devices by JAX's collectives and lax.ppermute only.
A program may use at most 64 MiB of HBM per device.

v0:
```python
import jax
import jax.numpy as jnp
from jax import lax
from jax.sharding import PartitionSpec as P

HEADS = 64
KV_HEADS = 8
HD = 128
CAP = 2


neg_big = -1e30


def slot_ranks(route_rows):
    row_count = route_rows.shape[-1]
    order_ids = jnp.arange(row_count, dtype=jnp.int32)
    earlier = order_ids[:, None] > order_ids[None, :]
    same_route = route_rows[..., :, None] == route_rows[..., None, :]
    return jnp.sum(jnp.logical_and(same_route, earlier), axis=-1)


def prompt_scores(query_slots, key_slots, live_rows, factor):
    scores = (
        jnp.einsum(
            "scjhgd,schdl->scjhgl", query_slots, key_slots, preferred_element_type=jnp.float32
        )
        * factor
    )
    return jnp.where(live_rows[:, :, None, None, None, :], scores, neg_big)


def fresh_scores(query_slots, fresh_keys, factor):
    scores = (
        jnp.einsum(
            "scjhgd,scihd->scjhgi", query_slots, fresh_keys, preferred_element_type=jnp.float32
        )
        * factor
    )
    step_count = scores.shape[-1]
    causal = jnp.arange(step_count)[None, :] <= jnp.arange(step_count)[:, None]
    return jnp.where(causal[None, None, :, None, None, :], scores, neg_big)


def per_device(prompt_tokens, kv_weight, routes, lengths, queries, new_kv):
    groups = lax.axis_size("group")
    sections = lax.axis_size("section")
    tensors = lax.axis_size("tensor")
    prompts_here, positions, feat_here = prompt_tokens.shape
    columns = kv_weight.shape[1]
    col_here = columns // tensors
    kv_here = col_here // (2 * HD)
    per_group = HEADS // KV_HEADS
    factor = HD ** (-0.5)
    flat_tokens = prompt_tokens.reshape(prompts_here * positions, feat_here)
    projected = lax.psum_scatter(
        lax.dot_general(
            kv_weight, flat_tokens, (((0,), (1,)), ((), ())), preferred_element_type=jnp.float32
        ).astype(jnp.bfloat16),
        "tensor",
        scatter_dimension=0,
        tiled=True,
    ).astype(jnp.float32)
    group_me = lax.axis_index("group")
    section_me = lax.axis_index("section")
    first_prompt = (group_me * sections + section_me) * prompts_here
    my_lengths = lax.dynamic_slice_in_dim(lengths, first_prompt, prompts_here, 0)
    my_routes = lax.dynamic_slice_in_dim(routes[:, 0], first_prompt, prompts_here, 0)
    position_ids = jnp.arange(positions, dtype=jnp.int32)
    live_prompt = position_ids[None, :] < my_lengths[:, None]
    keyvals = jnp.where(
        live_prompt[None, :, :], projected.reshape(col_here, prompts_here, positions), 0.0
    ).astype(jnp.bfloat16)
    targets = my_routes * CAP + slot_ranks(my_routes)
    slot_ids = jnp.arange(groups * CAP, dtype=jnp.int32)
    placing_mask = targets[None, :] == slot_ids[:, None]
    placing = placing_mask.astype(jnp.bfloat16)
    outgoing = jnp.einsum(
        "sp,dpl->sdl", placing, keyvals, preferred_element_type=jnp.float32
    ).astype(jnp.bfloat16)
    outgoing = outgoing.reshape(groups, CAP, col_here, positions)
    arrived = lax.all_to_all(outgoing, "group", split_axis=0, concat_axis=0, tiled=True)
    step_count = queries.shape[4]
    query_slots = queries.reshape(groups, CAP, step_count, kv_here, per_group, HD)
    fresh_rows = new_kv.reshape(groups, CAP, step_count, kv_here, 2, HD)
    fresh_keys = fresh_rows[:, :, :, :, 0]
    fresh_vals = fresh_rows[:, :, :, :, 1]
    new_scores = fresh_scores(query_slots, fresh_keys, factor)
    new_top = jnp.max(new_scores, axis=-1)
    all_routes = routes[:, 0].reshape(groups, sections * prompts_here)
    all_lengths = lengths.reshape(groups, sections * prompts_here)
    section_routes = lax.dynamic_slice_in_dim(
        all_routes, section_me * prompts_here, prompts_here, 1
    )
    section_lengths = lax.dynamic_slice_in_dim(
        all_lengths, section_me * prompts_here, prompts_here, 1
    )
    arriving = section_routes == group_me
    rank_all = slot_ranks(section_routes)
    cap_ids = jnp.arange(CAP, dtype=jnp.int32)
    slot_hits = jnp.logical_and(
        arriving[:, None, :], rank_all[:, None, :] == cap_ids[None, :, None]
    )
    slot_length = jnp.sum(jnp.where(slot_hits, section_lengths[:, None, :], 0), axis=-1)
    cache_slots = arrived.reshape(groups, CAP, kv_here, 2, HD, positions)
    live_slots = position_ids[None, None, :] < slot_length[:, :, None]
    old_scores = prompt_scores(query_slots, cache_slots[:, :, :, 0], live_slots, factor)
    top_score = jnp.maximum(jnp.max(old_scores, axis=-1), new_top)
    old_weights = jnp.exp(old_scores - top_score[..., None])
    new_weights = jnp.exp(new_scores - top_score[..., None])
    weight_total = jnp.sum(old_weights, axis=-1) + jnp.sum(new_weights, axis=-1)
    summed = jnp.einsum(
        "scjhgl,schdl->scjhgd",
        old_weights.astype(jnp.bfloat16),
        cache_slots[:, :, :, 1],
        preferred_element_type=jnp.float32,
    )
    summed = summed + jnp.einsum(
        "scjhgi,scihd->scjhgd",
        new_weights.astype(jnp.bfloat16),
        fresh_vals,
        preferred_element_type=jnp.float32,
    )
    mixed = summed / weight_total[..., None]
    decode_cache = arrived.reshape(1, 1, groups, CAP, col_here, positions)
    attention = mixed.astype(jnp.bfloat16).reshape(
        1, 1, groups, CAP, step_count, kv_here * per_group * HD
    )
    return (decode_cache, attention)


def solution(mesh):
    return jax.shard_map(
        per_device,
        mesh=mesh,
        in_specs=(
            P(("group", "section"), None, "tensor"),
            P("tensor", None),
            P(),
            P(),
            P("group", "section", None, None, None, "tensor"),
            P("group", "section", None, None, None, "tensor"),
        ),
        out_specs=(
            P("group", "section", None, None, "tensor", None),
            P("group", "section", None, None, None, "tensor"),
        ),
        check_vma=False,
    )
```

profile of v0, /device:TPU:4, one launch (start us, length us, event | category | flops | bytes accessed | tf_op | source)
XLA Modules:
  0.0 153.0 jit_solution(11240863696243300814)
XLA Ops:
  7.2 0.0 reduce-scatter.2.cloned.1.call-start
  7.2 14.1 %convolution_convert_fusion = bf16[2048,2048]{1,0:T(8,128)(2,1)} fusion(bf16[1024,2048]{1,0:T(8,128)(2,1)} %param.7, bf16[2048,1024]{1,0:T(8,128)(2,1)} %bitcast.107), kind=kOutput, calls=%fused_computation | convolution fusion | flops 8594128896 | bytes 16777216 | tf_op jit(solution)/shard_map/dot_general | solution.py:57
  21.3 0.0 copy-start.3
  21.3 0.0 copy-start.2
  21.3 0.0 reduce-scatter.2.cloned.1.call-update
  21.3 0.6 copy-done.3
  22.0 0.1 dynamic_slice.16
  22.1 0.0 copy-done.2
  22.1 0.1 fusion.24
  22.1 0.2 convert_reduce_fusion.1
  22.3 0.1 multiply_add_fusion
  22.4 0.1 iota_compare_fusion.2
  22.5 57.0 %reduce-scatter.2.cloned.1.call-done = bf16[256,2048]{1,0:T(8,128)(2,1)} async-done(((bf16[2048,2048]{1,0:T(8,128)(2,1)}), bf16[256,2048]{1,0:T(8,128)(2,1)}) %reduce-scatter.2.cloned.1.call-update) | async-done | bytes 1048592 | tf_op jit(solution)/shard_map/reduce_scatter | solution.py:56
  79.5 1.4 copy.33
  80.9 0.3 fusion
  81.2 0.8 convolution_convert_fusion.1
  82.0 0.0 copy-start
  82.0 0.0 copy-start.1
  82.0 2.1 %copy.15 = bf16[16,2,256,128]{3,2,1,0:T(8,128)(2,1)} copy(bf16[16,2,256,128]{3,1,0,2:T(2,128)(2,1)S(1)} %bitcast.105) | data formatting | bytes 4194304 | tf_op jit(solution)/shard_map/reshape | solution.py:81
  84.2 7.7 %all-to-all-start = ((bf16[16,2,256,128]{3,2,1,0:T(8,128)(2,1)}), bf16[16,2,256,128]{3,2,1,0:T(8,128)(2,1)S(1)}, u32[]{:S(2)}, u32[]{:S(2)}) async-start(bf16[16,2,256,128]{3,2,1,0:T(8,128)(2,1)} %copy.15), calls=%async_computation.1 | async-start | bytes 4194304 | tf_op jit(solution)/shard_map/all_to_all | solution.py:82
  91.9 0.1 reshape.175
  92.0 0.0 copy-done
  92.0 0.1 reshape.177
  92.1 0.0 copy-done.1
  92.1 0.5 broadcast.60
  92.6 0.7 reduce.7
  93.3 0.1 reshape_squeeze.3
  93.4 0.1 constant_dynamic-slice_fusion
  93.5 0.1 broadcast_compare_fusion
  93.5 0.4 convert_reduce_fusion
  94.0 0.1 select_reduce_fusion
  94.1 0.1 copy.17
  94.2 0.1 iota_compare_fusion.1
  94.3 0.1 fusion.25
  94.4 1.3 fusion.27
  95.7 46.1 %all-to-all-done = bf16[16,2,256,128]{3,2,1,0:T(8,128)(2,1)S(1)} async-done(((bf16[16,2,256,128]{3,2,1,0:T(8,128)(2,1)}), bf16[16,2,256,128]{3,2,1,0:T(8,128)(2,1)S(1)}, u32[]{:S(2)}, u32[]{:S(2)}) %all-to-all-start) | async-done | bytes 2097184 | tf_op jit(solution)/shard_map/all_to_all | solution.py:82
  141.8 0.5 fusion.26
  142.3 0.3 fusion.15
  142.6 0.3 convolution_bitcast_fusion
  142.9 0.5 fusion.10
  143.3 0.7 fusion.9
  144.1 0.8 reshape.183
  144.8 1.3 copy.41
  (4 shorter events, 0.1 us)
Async XLA Ops:
  7.2 72.3 %reduce-scatter.2.cloned.1.call-start = ((), (), s32[]{:S(2)}) async-start(), calls=%async_computation.2 | async-start | bytes 9437184 | tf_op jit(solution)/shard_map/reduce_scatter | solution.py:56
  21.3 0.7 copy-start.3
  21.3 0.8 copy-start.2
  82.0 10.0 %copy-start = (bf16[1,1,16,2,4,1024]{5,4,3,2,1,0:T(4,128)(2,1)S(1)}, bf16[1,1,16,2,4,1024]{5,4,3,2,1,0:T(4,128)(2,1)}, u32[]{:S(2)}) copy-start(bf16[1,1,16,2,4,1024]{5,4,3,2,1,0:T(4,128)(2,1)} %param.10) | copy-start | bytes 786436
  82.0 10.1 %copy-start.1 = (bf16[1,1,16,2,4,256]{5,4,3,2,1,0:T(4,128)(2,1)S(1)}, bf16[1,1,16,2,4,256]{5,4,3,2,1,0:T(4,128)(2,1)}, u32[]{:S(2)}) copy-start(bf16[1,1,16,2,4,256]{5,4,3,2,1,0:T(4,128)(2,1)} %param.11) | copy-start | bytes 196612
  84.2 57.6 %all-to-all-start = ((bf16[16,2,256,128]{3,2,1,0:T(8,128)(2,1)}), bf16[16,2,256,128]{3,2,1,0:T(8,128)(2,1)S(1)}, u32[]{:S(2)}, u32[]{:S(2)}) async-start(bf16[16,2,256,128]{3,2,1,0:T(8,128)(2,1)} %copy.15), calls=%async_computation.1 | async-start | bytes 4194304 | tf_op jit(solution)/shard_map/all_to_all | solution.py:82
Sparse Core Ops, SparseCore 0:
  21.5 57.9 reduce-scatter.1
where the time goes:
time: 154 us; the launch traced here: 153 us
  waiting for transfers between devices  103 us (67%)
  matrix products  17.7 us (11%)
  between operations  14.2 us (9%)
  starting transfers between devices  7.76 us (5%)
  local copies, waits for them, and re-layouts  7.54 us (5%)
  other arithmetic  2.74 us (2%)
    reduce_scatter x1, waiting for transfers between devices, per_device(): lax.psum_scatter(lax.dot_general(kv_weight, flat_tokens, (((0,), (1,)), (...  57 us
    all_to_all x1, waiting for transfers between devices, per_device(): lax.all_to_all(outgoing, 'group', split_axis=0, concat_axis=0, tiled=True)  46.1 us
    dot_general x1, matrix products, per_device(): lax.dot_general(kv_weight, flat_tokens, (((0,), (1,)), ((), ())), preferr...  14.1 us
    all_to_all x1, starting transfers between devices, per_device(): lax.all_to_all(outgoing, 'group', split_axis=0, concat_axis=0, tiled=True)  7.73 us
    unnamed x11, local copies, waits for them, and re-layouts  3.94 us
  transfers between devices with their start and end apart: 2, of which 2 were waited for; matrix products, arithmetic and copies ran while one was open for 3% of the time, Pallas kernels for 0%

commit v1 on v0

v1 whole, which is shorter than its diff:
```python
import functools

import jax
import jax.numpy as jnp
from jax import lax
from jax.experimental import pallas as pl
from jax.experimental.pallas import tpu as pltpu
from jax.sharding import PartitionSpec as P

HEADS = 64
KV_HEADS = 8
HD = 128
CAP = 2
TILE = 256
DIRECT = (1, 7)
FAR_FIRST = (4, 3, 5, 2, 6)
FORWARD = ((0, 4, 3, 5), (2, 6))
PLACE_FLOPS = (0, 30_000_000_000, 30_000_000_000)

neg_big = -1e30
VMEM_LIMIT = 24 * 1024 * 1024
CONTRACT_LAST = (((1,), (1,)), ((), ()))


def vmem_specs(count):
    return [pl.BlockSpec(memory_space=pltpu.VMEM)] * count


def smem_specs(count):
    return [pl.BlockSpec(memory_space=pltpu.SMEM)] * count


def any_specs(count):
    return [pl.BlockSpec(memory_space=pl.ANY)] * count


def shaped(*shape, dtype=jnp.bfloat16):
    return jax.ShapeDtypeStruct(shape, dtype)


def project_kernel(split, mine, info_ref, tokens_ref, weight_ref, *refs):
    came_ref, out_refs = (refs[0], refs[1:]) if mine else (None, refs)
    ys = weight_ref.shape[1] // (4 * HD)
    y, core = info_ref[0], info_ref[1]
    side = core if mine else 1 - core
    starts = [
        (lax.rem(y + d, ys) * 2 + side) * (2 * HD) + (0 if split else HD) for d in range(ys)
    ]
    cols = [pl.ds(pl.multiple_of(start, HD), HD) for start in starts]
    count = tokens_ref.shape[0]
    low = lax.broadcasted_iota(jnp.int32, (TILE, HD), 1) < HD // 2

    def product(first):
        heads = jnp.concatenate([weight_ref[:, col] for col in cols], axis=1)
        tokens = tokens_ref[first : first + TILE, :]
        return jnp.dot(tokens, heads, preferred_element_type=jnp.float32)

    def put(part, d, rows, block):
        if mine:
            block = block + came_ref[part * ys + d, rows, :].astype(jnp.float32)
            out_refs[part * ys + d][rows, :] = block.astype(jnp.bfloat16)
        else:
            out_refs[0][part * ys + d, rows, :] = block.astype(jnp.bfloat16)

    for first in range(0, count // 2 if split else count, TILE):
        rows = slice(first, first + TILE)
        here = product(first)
        there = product(first + count // 2) if split else None
        for d in range(ys):
            block = here[:, d * HD : (d + 1) * HD]
            if split:
                beside = there[:, d * HD : (d + 1) * HD]
                put(0, d, rows, jnp.where(low, block, pltpu.roll(beside, HD // 2, 1)))
                put(1, d, rows, jnp.where(low, pltpu.roll(block, HD // 2, 1), beside))
            else:
                put(0, d, rows, block)


def place_kernel(relative, info_ref, routes_ref, lengths_ref, *refs):
    sum_refs, out_refs = refs[:4], refs[4:-4]
    taken_ref, prompt_ref, live_ref, turned_ref = refs[-4:]
    me, first = info_ref[2], info_ref[3]
    groups, slots = taken_ref.shape[0], prompt_ref.shape[0]
    prompts = turned_ref.shape[0]
    for r in range(groups):
        taken_ref[r] = 0
    for s in range(slots):
        prompt_ref[s] = 0
        live_ref[s] = 0
    for p in range(prompts):
        route = routes_ref[first + p]
        rank = taken_ref[route]
        taken_ref[route] = rank + 1
        way = route
        if relative:
            ahead = lax.rem(route // 2 - me // 2 + groups // 2, groups // 2)
            way = ahead * 2 + lax.rem(route + me, 2)
        prompt_ref[way * CAP + rank] = p
        live_ref[way * CAP + rank] = lengths_ref[first + p]
    cols = turned_ref.shape[1]
    abreast = HD // cols
    for p in range(prompts // abreast):
        rows = slice(p * HD, (p + 1) * HD)
        total = sum_refs[0][rows, :].astype(jnp.float32)
        for came in sum_refs[1:]:
            total = total + came[rows, :].astype(jnp.float32)
        turned = total.T.astype(jnp.bfloat16)
        for i in range(abreast):
            turned_ref[p + i * (prompts // abreast)] = turned[i * cols : (i + 1) * cols]
    place_ids = lax.broadcasted_iota(jnp.int32, (cols, HD), 1)
    ways = ways_of(out_refs, groups // 2) if relative else {}
    for s in range(slots):
        block = turned_ref[prompt_ref[s]]
        block = jnp.where(place_ids < live_ref[s], block, jnp.zeros_like(block))
        if relative:
            ways[s // (2 * CAP), s // CAP % 2][s % CAP] = block
        else:
            out_refs[0][s] = block


def ways_of(refs, zs):
    found = {}
    at = 0
    for d in range(zs):
        for e in range(2):
            found[d, e] = refs[at] if d in DIRECT else refs[at].at[e]
            at += 1 if d in DIRECT or e else 0
    return found


def halves_kernel(*refs):
    for i, piece in enumerate(refs[:-1]):
        refs[-1][i] = piece[1]


def score_kernel(steps, info_ref, routes_ref, lengths_ref, query_ref, fresh_ref, *refs):
    keys_refs, (cache_ref, weight_ref, scale_ref, fresh_out_ref, live_ref, sems) = refs[:2], refs[2:]
    cols = HD // len(keys_refs)
    copies = []
    for i, keys_ref in enumerate(keys_refs):
        rows = slice(i * cols, (i + 1) * cols)
        copies.append(pltpu.make_async_copy(keys_ref, cache_ref.at[:, rows, :], sems.at[i]))
        copies[-1].start()
    me, section, sections = info_ref[2], info_ref[4], info_ref[5]
    slots, rows = query_ref.shape[0], query_ref.shape[1]
    groups = slots // CAP
    prompts = routes_ref.shape[0] // (groups * 2)

    def count(source, carry):
        first = (source * sections + section) * prompts
        found = jnp.int32(0)
        for p in range(prompts):
            live_ref[source * (CAP + 1) + found] = lengths_ref[first + p]
            found = found + jnp.where(routes_ref[first + p] == me, 1, 0)
        for c in range(CAP):
            at = source * (CAP + 1) + c
            live_ref[at] = jnp.where(c < found, live_ref[at], 0)
        return carry

    lax.fori_loop(0, groups, count, 0)
    factor = HD ** (-0.5)
    place_ids = lax.broadcasted_iota(jnp.int32, (rows, HD), 1)
    batch = 4
    many = batch * rows
    row_ids = lax.broadcasted_iota(jnp.int32, (many, batch * steps), 0)
    fresh_ids = lax.broadcasted_iota(jnp.int32, (many, batch * steps), 1)
    seen = jnp.logical_and(
        row_ids // rows == fresh_ids // steps,
        fresh_ids % steps <= row_ids % rows // (rows // steps),
    )
    for start in range(0, slots, batch):
        group = slice(start, start + batch)
        query = query_ref[group].reshape(many, HD)
        fresh = fresh_ref[group].reshape(batch * steps, 2 * HD)
        new = lax.dot_general(
            query, fresh[:, :HD], CONTRACT_LAST, preferred_element_type=jnp.float32
        )
        new = jnp.where(seen, new * factor, neg_big)
        olds = []
        for s in range(start, start + batch):
            keys = jnp.concatenate([keys_ref[s] for keys_ref in keys_refs], axis=0)
            old = jnp.dot(query_ref[s], keys, preferred_element_type=jnp.float32)
            live = live_ref[s + s // CAP]
            olds.append(jnp.where(place_ids < live, old * factor, neg_big))
        old = jnp.concatenate(olds, axis=0)
        top = jnp.maximum(
            jnp.max(old, axis=-1, keepdims=True), jnp.max(new, axis=-1, keepdims=True)
        )
        old = jnp.exp(old - top)
        new = jnp.exp(new - top)
        total = jnp.sum(old, axis=-1, keepdims=True) + jnp.sum(new, axis=-1, keepdims=True)
        scale = jnp.broadcast_to(1.0 / total, (many, HD))
        fresh_out = jnp.dot(
            new.astype(jnp.bfloat16), fresh[:, HD:], preferred_element_type=jnp.float32
        )
        weight_ref[group] = old.astype(jnp.bfloat16).reshape(batch, rows, HD)
        scale_ref[group] = scale.reshape(batch, rows, HD)
        fresh_out_ref[group] = (fresh_out * scale).reshape(batch, rows, HD)
    for copy in copies:
        copy.wait()


def mix_kernel(zs, info_ref, weight_ref, scale_ref, fresh_out_ref, *refs):
    near = zs + len(DIRECT)
    cache_ref, out_ref, sems = refs[near + len(FORWARD) + 1 :]
    ways = ways_of(refs[:near], zs)
    for order, group_ref in zip(FORWARD, refs[near:]):
        for i, d in enumerate(order):
            ways[d, 1] = group_ref.at[i]
    me = info_ref[2]
    copies = []
    for i, ((d, e), vals_ref) in enumerate(ways.items()):
        source = lax.rem(me // 2 - d + zs, zs) * 2 + lax.rem(me + e, 2)
        slots = pl.ds(source * CAP, CAP)
        copies.append(pltpu.make_async_copy(vals_ref, cache_ref.at[slots, HD:, :], sems.at[i]))
        copies[-1].start()
        for c in range(CAP):
            slot = source * CAP + c
            summed = lax.dot_general(
                weight_ref[slot], vals_ref[c], CONTRACT_LAST, preferred_element_type=jnp.float32
            )
            mixed = summed * scale_ref[slot] + fresh_out_ref[slot]
            out_ref[slot] = mixed.astype(jnp.bfloat16)
    for copy in copies:
        copy.wait()


def per_device(prompt_tokens, kv_weight, routes, lengths, queries, new_kv):
    groups = lax.axis_size("group")
    sections = lax.axis_size("section")
    tensors = lax.axis_size("tensor")
    prompts_here, positions, feat_here = prompt_tokens.shape
    columns = kv_weight.shape[1]
    col_here = columns // tensors
    step_count = queries.shape[4]
    per_group = HEADS // KV_HEADS
    rows = step_count * per_group
    slots = groups * CAP
    ys = tensors // 2
    token_count = prompts_here * positions
    group_me = lax.axis_index("group")
    section_me = lax.axis_index("section")
    tensor_me = lax.axis_index("tensor")
    first_prompt = (group_me * sections + section_me) * prompts_here
    info = jnp.stack(
        [tensor_me // 2, tensor_me % 2, group_me]
        + [first_prompt, section_me, jnp.int32(sections)]
    ).astype(jnp.int32)
    core_pairs = [(t, t ^ 1) for t in range(tensors)]
    y_pairs = [
        [(y * 2 + c, (y + d) % ys * 2 + c) for y in range(ys) for c in range(2)] for d in range(ys)
    ]
    zs = groups // 2
    z_pairs = {
        (d, e): [
            (z * 2 + x, (z + d) % zs * 2 + (x + e) % 2) for z in range(zs) for x in range(2)
        ]
        for d in range(zs)
        for e in range(2)
    }
    flat_tokens = prompt_tokens.reshape(token_count, feat_here)
    flat_routes = routes[:, 0]
    params = pltpu.CompilerParams(vmem_limit_bytes=VMEM_LIMIT)

    def call(kernel, **options):
        return pl.pallas_call(kernel, compiler_params=params, **options)


    came = []
    for split in (True, False):
        sent = call(
            functools.partial(project_kernel, split, False),
            in_specs=smem_specs(1) + vmem_specs(2),
            out_specs=vmem_specs(1)[0],
            out_shape=shaped(*((2 * ys, token_count // 2) if split else (ys, token_count)), HD),
        )(info, flat_tokens, kv_weight)
        came.append(lax.ppermute(sent, "tensor", core_pairs))
    sums = []
    for split in (True, False):
        made = call(
            functools.partial(project_kernel, split, True),
            in_specs=smem_specs(1) + vmem_specs(3),
            out_specs=vmem_specs(2 * ys if split else ys),
            out_shape=[shaped(token_count // 2, HD)] * (2 * ys)
            if split
            else [shaped(token_count, HD)] * ys,
        )(info, flat_tokens, kv_weight, came[0 if split else 1])
        sums += [made[:ys], made[ys:]] if split else [made]
    summed = []
    for part in sums:
        if summed:
            part, summed[-1][1] = lax.optimization_barrier((part, summed[-1][1]))
        summed.append(
            [part[0]] + [lax.ppermute(part[d], "tensor", y_pairs[d]) for d in (2, 1, 3)]
        )

    def place(part, relative, out_shape):
        return call(
            functools.partial(place_kernel, relative),
            in_specs=smem_specs(3) + vmem_specs(ys),
            out_specs=vmem_specs(len(out_shape)),
            out_shape=out_shape,
            scratch_shapes=[
                pltpu.SMEM((groups,), jnp.int32),
                pltpu.SMEM((slots,), jnp.int32),
                pltpu.SMEM((slots,), jnp.int32),
                pltpu.VMEM((prompts_here, out_shape[0].shape[-2], HD), jnp.bfloat16),
            ],
            cost_estimate=pl.CostEstimate(
                flops=PLACE_FLOPS[part], bytes_accessed=0, transcendentals=0
            ),
        )(info, flat_routes, lengths, *summed[part])

    keys = []
    for part in range(2):
        (placed,) = place(part, False, [shaped(slots, HD // 2, positions)])
        keys.append(lax.all_to_all(placed, "group", 0, 0, tiled=True))
    shapes = []
    for d in range(zs):
        shapes += [shaped(CAP, HD, positions)] * 2 if d in DIRECT else [
            shaped(2, CAP, HD, positions)
        ]
    placed = iter(place(2, True, shapes))
    pieces = {}
    for d in range(zs):
        pieces[d] = [next(placed), next(placed)] if d in DIRECT else next(placed)
    for d in FAR_FIRST:
        pieces[d] = lax.ppermute(pieces[d], "group", z_pairs[d, 0])
    for d in DIRECT:
        pieces[d] = [lax.ppermute(pieces[d][e], "group", z_pairs[d, e]) for e in range(2)]
    cache, weights, scales, fresh_out = call(
        functools.partial(score_kernel, step_count),
        in_specs=smem_specs(3) + vmem_specs(4),
        out_specs=any_specs(1) + vmem_specs(3),
        out_shape=[
            shaped(slots, col_here, positions),
            shaped(slots, rows, HD),
            shaped(slots, rows, HD, dtype=jnp.float32),
            shaped(slots, rows, HD, dtype=jnp.float32),
        ],
        scratch_shapes=[
            pltpu.SMEM((groups * (CAP + 1),), jnp.int32),
            pltpu.SemaphoreType.DMA((2,)),
        ],
    )(
        info,
        flat_routes,
        lengths,
        queries.reshape(slots, rows, HD),
        new_kv.reshape(slots, step_count, 2 * HD),
        *keys,
    )
    weights, far = lax.optimization_barrier((weights, pieces[FAR_FIRST[0]]))
    pieces[FAR_FIRST[0]] = far
    passed = []
    for order in FORWARD:
        halves = call(
            halves_kernel,
            in_specs=vmem_specs(len(order)),
            out_specs=vmem_specs(1)[0],
            out_shape=shaped(len(order), CAP, HD, positions),
        )(*[pieces[d] for d in order])
        passed.append(lax.ppermute(halves, "group", z_pairs[0, 1]))
    vals = []
    for d in range(zs):
        vals += pieces[d] if d in DIRECT else [pieces[d]]
    vals += passed

    cache, attention = call(
        functools.partial(mix_kernel, zs),
        in_specs=smem_specs(1) + vmem_specs(3 + len(vals)) + any_specs(1),
        out_specs=any_specs(1) + vmem_specs(1),
        out_shape=[shaped(slots, col_here, positions), shaped(slots, rows, HD)],
        scratch_shapes=[pltpu.SemaphoreType.DMA((groups,))],
        input_output_aliases={4 + len(vals): 0},
    )(info, weights, scales, fresh_out, *vals, cache)
    return (
        cache.reshape(1, 1, groups, CAP, col_here, positions),
        attention.reshape(1, 1, groups, CAP, step_count, per_group * HD),
    )


def solution(mesh):
    return jax.shard_map(
        per_device,
        mesh=mesh,
        in_specs=(
            P(("group", "section"), None, "tensor"),
            P("tensor", None),
            P(),
            P(),
            P("group", "section", None, None, None, "tensor"),
            P("group", "section", None, None, None, "tensor"),
        ),
        out_specs=(
            P("group", "section", None, None, "tensor", None),
            P("group", "section", None, None, None, "tensor"),
        ),
        check_vma=False,
    )
```

time: 154 us -> 115 us (0.75)
  waiting for transfers between devices: 103 us -> 29.7 us
  starting transfers between devices: 7.76 us -> 52.9 us
  Pallas kernels: 0 us -> 26.1 us
  matrix products: 17.7 us -> 0 us
  between operations: 14.2 us -> 0.84 us
  other arithmetic: 2.74 us -> 0 us
  local copies, waits for them, and re-layouts: 7.54 us -> 5.35 us
    reduce_scatter x1 -> x0, waiting for transfers between devices: 57 us -> none  [per_device(): lax.psum_scatter(lax.dot_general(kv_weight, flat_tokens, (((0,), (1,)), (...]
    ppermute x0 -> x22, starting transfers between devices: none -> 40.1 us  [the longest x9 16.3 us: per_device(): lax.ppermute(part[d], 'tensor', y_pairs[d])]
    all_to_all x1 -> x2, waiting for transfers between devices: 46.1 us -> 9.53 us  [per_device(): keys.append(lax.all_to_all(placed, 'group', 0, 0, tiled=True))]
    pallas_call x0 -> x11, Pallas kernels: none -> 26.1 us  [the longest x2 7.67 us: per_device(): call(functools.partial(project_kernel, split, True), in_specs=smem_specs(...]
    ppermute x0 -> x22, waiting for transfers between devices: none -> 20.1 us  [the longest x9 9.53 us: per_device(): lax.ppermute(part[d], 'tensor', y_pairs[d])]
    dot_general x6 -> x0, matrix products: 17.7 us -> none  [the longest x1 14.1 us: per_device(): lax.dot_general(kv_weight, flat_tokens, (((0,), (1,)), ((), ())), preferr...]
    all_to_all x1 -> x2, starting transfers between devices: 7.73 us -> 12.8 us  [per_device(): keys.append(lax.all_to_all(placed, 'group', 0, 0, tiled=True))]
    reshape x4 -> x2, local copies, waits for them, and re-layouts: 3.02 us -> 0.87 us  [the longest x1 0.77 us: per_device(): attention.reshape(1, 1, groups, CAP, step_count, per_group * HD)]
  transfers between devices with their start and end apart: 2 -> 24, of which waited for: 2 -> 10; matrix products, arithmetic and copies ran while one was open for 3% -> 0% of each run, Pallas kernels for 0% -> 18%
where the time goes in v1:
time: 115 us
  starting transfers between devices  52.9 us (46%)
  waiting for transfers between devices  29.7 us (26%)
  Pallas kernels  26.1 us (23%)
  local copies, waits for them, and re-layouts  5.35 us (5%)
    ppermute x9, starting transfers between devices, per_device(): lax.ppermute(part[d], 'tensor', y_pairs[d])  16.3 us
    ppermute x5, starting transfers between devices, per_device(): pieces[d] = lax.ppermute(pieces[d], 'group', z_pairs[d, 0])  14.9 us
    all_to_all x2, starting transfers between devices, per_device(): keys.append(lax.all_to_all(placed, 'group', 0, 0, tiled=True))  12.8 us
    all_to_all x2, waiting for transfers between devices, per_device(): keys.append(lax.all_to_all(placed, 'group', 0, 0, tiled=True))  9.53 us
    ppermute x9, waiting for transfers between devices, per_device(): lax.ppermute(part[d], 'tensor', y_pairs[d])  9.53 us
    pallas_call x2, Pallas kernels, per_device(): call(functools.partial(project_kernel, split, True), in_specs=smem_specs(...  7.67 us
    pallas_call x2, Pallas kernels, per_device(): call(functools.partial(project_kernel, split, False), in_specs=smem_specs...  6.7 us
    pallas_call x3, Pallas kernels, place(): call(functools.partial(place_kernel, relative), in_specs=smem_specs(3) +...  6.02 us
  transfers between devices with their start and end apart: 24, of which 10 were waited for; matrix products, arithmetic and copies ran while one was open for 0% of the time, Pallas kernels for 18%

profile of v1, /device:TPU:4, one launch (start us, length us, event | category | flops | bytes accessed | tf_op | source)
XLA Modules:
  0.0 114.8 jit_solution(17576606782182608167)
XLA Ops:
  0.7 0.1 stack.23.info_ref
  0.7 2.2 %copy-done = bf16[16,128,1024]{2,1,0:T(8,128)(2,1)S(1)} copy-done((bf16[16,128,1024]{2,1,0:T(8,128)(2,1)S(1)}, bf16[16,128,1024]{2,1,0:T(8,128)(2,1)}, u32[]{:S(2)}) %copy-start) | copy-done | bytes 4194328
  2.9 2.2 %copy-done.1 = bf16[1024,2048]{1,0:T(8,128)(2,1)S(1)} copy-done((bf16[1024,2048]{1,0:T(8,128)(2,1)S(1)}, bf16[1024,2048]{1,0:T(8,128)(2,1)}, u32[]{:S(2)}) %copy-start.1) | copy-done | bytes 4194328
  5.1 3.5 %shard_map.77 = bf16[8,1024,128]{2,1,0:T(8,128)(2,1)S(1)} custom-call(s32[6]{0:T(128)S(1)} %stack.23.info_ref, bf16[2048,1024]{1,0:T(8,128)(2,1)S(1)} %bitcast.9, bf16[1024,2048]{1,0:T(8,128)(2,1)S(1)} %copy-done.1), custom_call_target="tpu_custom_call" | custom-call | tf_op jit(solution)/shard_map/pallas_call | solution.py:271
  8.6 0.1 collective-permute-start
  8.7 3.2 %shard_map.80 = bf16[4,2048,128]{2,1,0:T(8,128)(2,1)S(1)} custom-call(s32[6]{0:T(128)S(1)} %stack.23.info_ref, bf16[2048,1024]{1,0:T(8,128)(2,1)S(1)} %bitcast.10, bf16[1024,2048]{1,0:T(8,128)(2,1)S(1)} %copy-done.1), custom_call_target="tpu_custom_call" | custom-call | tf_op jit(solution)/shard_map/pallas_call | solution.py:271
  11.9 0.6 collective-permute-start.4
  12.5 0.3 collective-permute-done.refs_0_
  12.8 4.3 %shard_map.78 = (bf16[1024,128]{1,0:T(8,128)(2,1)S(1)}, bf16[1024,128]{1,0:T(8,128)(2,1)S(1)}, bf16[1024,128]{1,0:T(8,128)(2,1)S(1)}, bf16[1024,128]{1,0:T(8,128...) custom-call(s32[6]{0:T(128)S(1)} %stack.23.info_ref, ...), custom_call_target="tpu_custom_call" | custom-call | tf_op jit(solution)/shard_map/pallas_call | solution.py:280
  17.2 3.2 %collective-permute-start.1 = (bf16[1024,128]{1,0:T(8,128)(2,1)S(1)}, bf16[1024,128]{1,0:T(8,128)(2,1)S(1)}, u32[]{:S(2)}, u32[]{:S(2)}) collective-permute-start(bf16[1024,128]{1,0:T(8,128)(2,1)S(1)} %get-tuple-element.47), channel_id=1, source_target_pairs={{0,4},{1,5},{2,6},{3,7},{4,0},{5,1},{6,2},{7,3},{8,12},{9,13},{10,... | collective-permute-start | bytes 786440 | tf_op jit(solution)/shard_map/ppermute | solution.py:294
  20.4 0.7 collective-permute-start.2
  21.0 2.6 %collective-permute-start.3 = (bf16[1024,128]{1,0:T(8,128)(2,1)S(1)}, bf16[1024,128]{1,0:T(8,128)(2,1)S(1)}, u32[]{:S(2)}, u32[]{:S(2)}) collective-permute-start(bf16[1024,128]{1,0:T(8,128)(2,1)S(1)} %get-tuple-element.50), channel_id=1, source_target_pairs={{0,6},{1,7},{2,0},{3,1},{4,2},{5,3},{6,4},{7,5},{8,14},{9,15},{10,... | collective-permute-start | bytes 786440 | tf_op jit(solution)/shard_map/ppermute | solution.py:294
  23.6 4.3 %collective-permute-done.1.refs_1_ = bf16[1024,128]{1,0:T(8,128)(2,1)S(1)} collective-permute-done((bf16[1024,128]{1,0:T(8,128)(2,1)S(1)}, bf16[1024,128]{1,0:T(8,128)(2,1)S(1)}, u32[]{:S(2)}, u32[]{:S(2)}) %collective-permute-start.1) | collective-permute-done | bytes 262176 | tf_op jit(solution)/shard_map/ppermute | solution.py:294
  27.9 3.2 %collective-permute-start.5 = (bf16[1024,128]{1,0:T(8,128)(2,1)}, bf16[1024,128]{1,0:T(8,128)(2,1)}, u32[]{:S(2)}, u32[]{:S(2)}) collective-permute-start(bf16[1024,128]{1,0:T(8,128)(2,1)} %get-tuple-element.56), channel_id=1, source_target_pairs={{0,4},{1,5},{2,6},{3,7},{4,0},{5,1},{6,2},{7,3},{8,12},{9,13},{10,... | collective-permute-start | bytes 786440 | tf_op jit(solution)/shard_map/ppermute | solution.py:294
  31.1 0.7 collective-permute-start.6
  31.8 0.0 collective-permute-done.4.refs_0_
  31.8 2.6 %collective-permute-start.7 = (bf16[1024,128]{1,0:T(8,128)(2,1)S(1)}, bf16[1024,128]{1,0:T(8,128)(2,1)}, u32[]{:S(2)}, u32[]{:S(2)}) collective-permute-start(bf16[1024,128]{1,0:T(8,128)(2,1)S(1)} %get-tuple-element.59), channel_id=1, source_target_pairs={{0,6},{1,7},{2,0},{3,1},{4,2},{5,3},{6,4},{7,5},{8,14},{9,15},{10,... | collective-permute-start | bytes 786440 | tf_op jit(solution)/shard_map/ppermute | solution.py:294
  34.3 3.3 %shard_map.81 = (bf16[2048,128]{1,0:T(8,128)(2,1)S(1)}, bf16[2048,128]{1,0:T(8,128)(2,1)S(1)}, bf16[2048,128]{1,0:T(8,128)(2,1)S(1)}, bf16[2048,128]{1,0:T(8,128)(2,1)S(1)}) custom-call(s32[6]{0:T(128)S(1)} %stack.23.info_ref, bf16[2048,1024]{1,0:T(8,128)(2,1)S(1)} %bitcast.12, bf16[1024,2048]{1,0:T(8,128)(2,1)S(1)} %copy-done.1, ...), custom_call_target="tpu_custom_call" | custom-call | tf_op jit(solution)/shard_map/pallas_call | solution.py:280
  37.6 0.0 collective-permute-done.2.refs_2_
  37.7 0.0 collective-permute-done.3.refs_3_
  37.7 1.7 %shard_map.79 = bf16[32,64,128]{2,1,0:T(8,128)(2,1)} custom-call(s32[6]{0:T(128)S(1)} %stack.23.info_ref, s32[512]{0:T(512)S(1)} %bitcast.14, s32[512]{0:T(512)S(1)} %copy-done.4, bf16[1024,128]{1,0:T(8,128)(2,1)S(1)} %get-tuple-element.42.refs_0_, bf16[1024,128]{1,0:T(8,128)(2,1)S(1)} %collective-permute-done.1.refs_1_, ...), custom_call_target="tpu_custom_call" | custom-call | tf_op jit(solution)/shard_map/pallas_call | solution.py:298
  39.4 9.2 %all-to-all-start = ((bf16[32,64,128]{2,1,0:T(8,128)(2,1)}), bf16[32,64,128]{2,1,0:T(8,128)(2,1)S(1)}, u32[]{:S(2)}, u32[]{:S(2)}) async-start(bf16[32,64,128]{2,1,0:T(8,128)(2,1)} %shard_map.79), calls=%async_computation | async-start | bytes 1048576 | tf_op jit(solution)/shard_map/all_to_all | solution.py:317
  48.6 0.0 collective-permute-done.5.refs_1_
  48.6 0.1 collective-permute-start.8
  48.7 0.8 collective-permute-start.9
  49.6 2.5 %collective-permute-start.10 = (bf16[2048,128]{1,0:T(8,128)(2,1)S(1)}, bf16[2048,128]{1,0:T(8,128)(2,1)}, u32[]{:S(2)}, u32[]{:S(2)}) collective-permute-start(bf16[2048,128]{1,0:T(8,128)(2,1)S(1)} %get-tuple-element.64), channel_id=1, source_target_pairs={{0,6},{1,7},{2,0},{3,1},{4,2},{5,3},{6,4},{7,5},{8,14},{9,15},{10,... | collective-permute-start | bytes 1572872 | tf_op jit(solution)/shard_map/ppermute | solution.py:294
  52.0 0.0 collective-permute-done.6.refs_2_
  52.1 0.0 collective-permute-done.7.refs_3_
  52.1 2.2 %shard_map.82 = bf16[32,64,128]{2,1,0:T(8,128)(2,1)} custom-call(s32[6]{0:T(128)S(1)} %stack.23.info_ref, s32[512]{0:T(512)S(1)} %bitcast.15, s32[512]{0:T(512)S(1)} %copy-done.4, bf16[1024,128]{1,0:T(8,128)(2,1)S(1)} %get-tuple-element.51.refs_0_, bf16[1024,128]{1,0:T(8,128)(2,1)} %collective-permute-done.5.refs_1_, ...), custom_call_target="tpu_custom_call" | custom-call | flops 30000001024 | tf_op jit(solution)/shard_map/pallas_call | solution.py:298
  54.3 9.5 %all-to-all-done.refs_0_ = bf16[32,64,128]{2,1,0:T(8,128)(2,1)S(1)} async-done(((bf16[32,64,128]{2,1,0:T(8,128)(2,1)}), bf16[32,64,128]{2,1,0:T(8,128)(2,1)S(1)}, u32[]{:S(2)}, u32[]{:S(2)}) %all-to-all-start) | async-done | bytes 524320 | tf_op jit(solution)/shard_map/all_to_all | solution.py:317
  63.8 3.6 %all-to-all-start.1 = ((bf16[32,64,128]{2,1,0:T(8,128)(2,1)}), bf16[32,64,128]{2,1,0:T(8,128)(2,1)S(1)}, u32[]{:S(2)}, u32[]{:S(2)}) async-start(bf16[32,64,128]{2,1,0:T(8,128)(2,1)} %shard_map.82), calls=%async_computation.1 | async-start | bytes 1048576 | tf_op jit(solution)/shard_map/all_to_all | solution.py:317
  67.4 0.0 copy-start.5
  67.4 0.0 copy-start.2
  67.4 0.0 collective-permute-done.8.refs_1_
  67.4 5.2 %collective-permute-done.9.refs_2_ = bf16[2048,128]{1,0:T(8,128)(2,1)} collective-permute-done((bf16[2048,128]{1,0:T(8,128)(2,1)S(1)}, bf16[2048,128]{1,0:T(8,128)(2,1)}, u32[]{:S(2)}, u32[]{:S(2)}) %collective-permute-start.9) | collective-permute-done | bytes 524320 | tf_op jit(solution)/shard_map/ppermute | solution.py:294
  72.7 0.0 collective-permute-done.10.refs_3_
  72.7 2.1 %shard_map.84 = (bf16[2,2,128,128]{3,2,1,0:T(8,128)(2,1)S(1)}, bf16[2,128,128]{2,1,0:T(8,128)(2,1)S(1)}, bf16[2,128,128]{2,1,0:T(8,128)(2,1)S(1)}, bf16[2,2,128,...) custom-call(s32[6]{0:T(128)S(1)} %stack.23.info_ref, ...), custom_call_target="tpu_custom_call" | custom-call | flops 30000001024 | tf_op jit(solution)/shard_map/pallas_call | solution.py:298
  74.8 5.6 %collective-permute-start.11 = (bf16[2,2,128,128]{3,2,1,0:T(8,128)(2,1)S(1)}, bf16[2,2,128,128]{3,2,1,0:T(8,128)(2,1)S(1)}, u32[]{:S(2)}, u32[]{:S(2)}) collective-permute-start(bf16[2,2,128,128]{3,2,1,0:T(8,128)(2,1)S(1)} %get-tuple-element.65), channel_id=1, source_target_pairs={{0,128},{16,144},{32,160},{48,176},{64,192},{80,208},{96,224},{112... | collective-permute-start | bytes 393224 | tf_op jit(solution)/shard_map/ppermute | solution.py:328
  80.4 0.6 collective-permute-start.15
  81.0 4.5 %collective-permute-start.16 = (bf16[2,2,128,128]{3,2,1,0:T(8,128)(2,1)S(1)}, bf16[2,2,128,128]{3,2,1,0:T(8,128)(2,1)S(1)}, u32[]{:S(2)}, u32[]{:S(2)}) collective-permute-start(bf16[2,2,128,128]{3,2,1,0:T(8,128)(2,1)S(1)} %get-tuple-element.75), channel_id=1, source_target_pairs={{0,160},{16,176},{32,192},{48,208},{64,224},{80,240},{96,0},{112,1... | collective-permute-start | bytes 393224 | tf_op jit(solution)/shard_map/ppermute | solution.py:328
  85.4 0.1 reshape.19.query_ref
  85.5 0.6 collective-permute-start.14
  86.2 3.6 %collective-permute-start.17 = (bf16[2,2,128,128]{3,2,1,0:T(8,128)(2,1)S(1)}, bf16[2,2,128,128]{3,2,1,0:T(8,128)(2,1)S(1)}, u32[]{:S(2)}, u32[]{:S(2)}) collective-permute-start(bf16[2,2,128,128]{3,2,1,0:T(8,128)(2,1)S(1)} %get-tuple-element.76), channel_id=1, source_target_pairs={{0,192},{16,208},{32,224},{48,240},{64,0},{80,16},{96,32},{112,48}... | collective-permute-start | bytes 393224 | tf_op jit(solution)/shard_map/ppermute | solution.py:328
  89.8 0.0 all-to-all-done.1.refs_1_
  89.8 3.5 %shard_map.83 = (bf16[32,256,128]{2,1,0:T(8,128)(2,1)}, bf16[32,32,128]{2,1,0:T(8,128)(2,1)S(1)}, f32[32,32,128]{2,1,0:T(8,128)S(1)}, f32[32,32,128]{2,1,0:T(8,128)S(1)}) custom-call(s32[6]{0:T(128)S(1)} %stack.23.info_ref, s32[512]{0:T(512)S(1)} %bitcast.17, s32[512]{0:T(512)S(1)} %copy-done.4, bf16[32,32,128]{2,1,0:T(8,128)(2,1)S(1)} %reshape.19.query_ref, ...), custom_call_target="tpu_custom_call" | custom-call | tf_op jit(solution)/shard_map/pallas_call | solution.py:331
  93.3 0.0 collective-permute-done.11.refs_1_.refs_5_
  93.3 4.6 %collective-permute-done.15.refs_2_.refs_4_ = bf16[2,2,128,128]{3,2,1,0:T(8,128)(2,1)S(1)} collective-permute-done((bf16[2,2,128,128]{3,2,1,0:T(8,128)(2,1)S(1)}, bf16[2,2,128,128]{3,2,1,0:T(8,128)(2,1)S(1)}, u32[]{:S(2)}, u32[]{:S(2)}) %collective-permute-start.15) | collective-permute-done | bytes 131104 | tf_op jit(solution)/shard_map/ppermute | solution.py:328
  97.9 0.2 collective-permute-done.16.refs_3_.refs_6_
  98.1 1.5 %collective-permute-start.20 = (bf16[4,2,128,128]{3,2,1,0:T(8,128)(2,1)S(1)}, bf16[4,2,128,128]{3,2,1,0:T(8,128)(2,1)S(1)}, u32[]{:S(2)}, u32[]{:S(2)}) collective-permute-start(bf16[4,2,128,128]{3,2,1,0:T(8,128)(2,1)S(1)} %shard_map.85), channel_id=1, source_target_pairs={{0,16},{16,0},{32,48},{48,32},{64,80},{80,64},{96,112},{112,96},{1... | collective-permute-start | bytes 786440 | tf_op jit(solution)/shard_map/ppermute | solution.py:363
  99.7 0.8 collective-permute-start.12
  100.4 0.0 collective-permute-done.14.refs_0_.refs_3_
  100.4 0.6 collective-permute-done.17.refs_1_.refs_7_
  101.1 1.6 %collective-permute-start.21 = (bf16[2,2,128,128]{3,2,1,0:T(8,128)(2,1)S(1)}, bf16[2,2,128,128]{3,2,1,0:T(8,128)(2,1)S(1)}, u32[]{:S(2)}, u32[]{:S(2)}) collective-permute-start(bf16[2,2,128,128]{3,2,1,0:T(8,128)(2,1)S(1)} %shard_map.86), channel_id=1, source_target_pairs={{0,16},{16,0},{32,48},{48,32},{64,80},{80,64},{96,112},{112,96},{1... | collective-permute-start | bytes 393224 | tf_op jit(solution)/shard_map/ppermute | solution.py:363
  102.6 1.5 %collective-permute-start.13 = (bf16[2,128,128]{2,1,0:T(8,128)(2,1)S(1)}, bf16[2,128,128]{2,1,0:T(8,128)(2,1)S(1)}, u32[]{:S(2)}, u32[]{:S(2)}) collective-permute-start(bf16[2,128,128]{2,1,0:T(8,128)(2,1)S(1)} %get-tuple-element.71), channel_id=1, source_target_pairs={{0,48},{16,32},{32,80},{48,64},{64,112},{80,96},{96,144},{112,128}... | collective-permute-start | bytes 196616 | tf_op jit(solution)/shard_map/ppermute | solution.py:330
  104.1 1.7 %collective-permute-start.18 = (bf16[2,128,128]{2,1,0:T(8,128)(2,1)S(1)}, bf16[2,128,128]{2,1,0:T(8,128)(2,1)S(1)}, u32[]{:S(2)}, u32[]{:S(2)}) collective-permute-start(bf16[2,128,128]{2,1,0:T(8,128)(2,1)S(1)} %get-tuple-element.77), channel_id=1, source_target_pairs={{0,224},{16,240},{32,0},{48,16},{64,32},{80,48},{96,64},{112,80},{... | collective-permute-start | bytes 196616 | tf_op jit(solution)/shard_map/ppermute | solution.py:330
  105.9 0.0 collective-permute-done.12.refs_1_
  105.9 1.1 %collective-permute-start.19 = (bf16[2,128,128]{2,1,0:T(8,128)(2,1)S(1)}, bf16[2,128,128]{2,1,0:T(8,128)(2,1)S(1)}, u32[]{:S(2)}, u32[]{:S(2)}) collective-permute-start(bf16[2,128,128]{2,1,0:T(8,128)(2,1)S(1)} %get-tuple-element.78), channel_id=1, source_target_pairs={{0,240},{16,224},{32,16},{48,0},{64,48},{80,32},{96,80},{112,64},{... | collective-permute-start | bytes 196616 | tf_op jit(solution)/shard_map/ppermute | solution.py:330
  107.0 2.3 %collective-permute-done.13.refs_2_ = bf16[2,128,128]{2,1,0:T(8,128)(2,1)S(1)} collective-permute-done((bf16[2,128,128]{2,1,0:T(8,128)(2,1)S(1)}, bf16[2,128,128]{2,1,0:T(8,128)(2,1)S(1)}, u32[]{:S(2)}, u32[]{:S(2)}) %collective-permute-start.13) | collective-permute-done | bytes 65568 | tf_op jit(solution)/shard_map/ppermute | solution.py:330
  109.4 0.0 collective-permute-done.18.refs_8_
  109.4 1.7 %collective-permute-done.19.refs_9_ = bf16[2,128,128]{2,1,0:T(8,128)(2,1)S(1)} collective-permute-done((bf16[2,128,128]{2,1,0:T(8,128)(2,1)S(1)}, bf16[2,128,128]{2,1,0:T(8,128)(2,1)S(1)}, u32[]{:S(2)}, u32[]{:S(2)}) %collective-permute-start.19) | collective-permute-done | bytes 65568 | tf_op jit(solution)/shard_map/ppermute | solution.py:330
  111.1 0.8 collective-permute-done.21.refs_11_
  111.9 0.0 collective-permute-done.20.refs_10_
  111.9 2.2 %shard_map.87 = (bf16[32,256,128]{2,1,0:T(8,128)(2,1)}, bf16[32,32,128]{2,1,0:T(8,128)(2,1)S(1)}) custom-call(s32[6]{0:T(128)S(1)} %stack.23.info_ref, bf16[32,32,128]{2,1,0:T(8,128)(2,1)S(1)} %get-tuple-element.66.weight_ref, f32[32,32,128]{2,1,0:T(8,128)S(1)} %get-tuple-element.67.scale_ref, ...), custom_call_target="tpu_custom_call", output_to_operand_aliasing={{0}: (16, {})} | custom-call | tf_op jit(solution)/shard_map/pallas_call | solution.py:369
  114.1 0.8 reshape.23
  (10 shorter events, 0.0 us)
Async XLA Ops:
  0.7 2.2 %copy-start = (bf16[16,128,1024]{2,1,0:T(8,128)(2,1)S(1)}, bf16[16,128,1024]{2,1,0:T(8,128)(2,1)}, u32[]{:S(2)}) copy-start(bf16[16,128,1024]{2,1,0:T(8,128)(2,1)} %param.6) | copy-start | bytes 12582916
  2.9 2.2 %copy-start.1 = (bf16[1024,2048]{1,0:T(8,128)(2,1)S(1)}, bf16[1024,2048]{1,0:T(8,128)(2,1)}, u32[]{:S(2)}) copy-start(bf16[1024,2048]{1,0:T(8,128)(2,1)} %weight_ref.7) | copy-start | bytes 12582916
  8.6 4.2 %collective-permute-start = (bf16[8,1024,128]{2,1,0:T(8,128)(2,1)S(1)}, bf16[8,1024,128]{2,1,0:T(8,128)(2,1)S(1)}, u32[]{:S(2)}, u32[]{:S(2)}) collective-permute-start(bf16[8,1024,128]{2,1,0:T(8,128)(2,1)S(1)} %shard_map.77), channel_id=1, source_target_pairs={{0,1},{1,0},{2,3},{3,2},{4,5},{5,4},{6,7},{7,6},{8,9},{9,8},{10,11... | collective-permute-start | bytes 6291464 | tf_op jit(solution)/shard_map/ppermute | solution.py:277
  11.9 19.8 %collective-permute-start.4 = (bf16[4,2048,128]{2,1,0:T(8,128)(2,1)S(1)}, bf16[4,2048,128]{2,1,0:T(8,128)(2,1)S(1)}, u32[]{:S(2)}, u32[]{:S(2)}) collective-permute-start(bf16[4,2048,128]{2,1,0:T(8,128)(2,1)S(1)} %shard_map.80), channel_id=1, source_target_pairs={{0,1},{1,0},{2,3},{3,2},{4,5},{5,4},{6,7},{7,6},{8,9},{9,8},{10,11... | collective-permute-start | bytes 6291464 | tf_op jit(solution)/shard_map/ppermute | solution.py:277
  17.2 10.7 %collective-permute-start.1 = (bf16[1024,128]{1,0:T(8,128)(2,1)S(1)}, bf16[1024,128]{1,0:T(8,128)(2,1)S(1)}, u32[]{:S(2)}, u32[]{:S(2)}) collective-permute-start(bf16[1024,128]{1,0:T(8,128)(2,1)S(1)} %get-tuple-element.47), channel_id=1, source_target_pairs={{0,4},{1,5},{2,6},{3,7},{4,0},{5,1},{6,2},{7,3},{8,12},{9,13},{10,... | collective-permute-start | bytes 786440 | tf_op jit(solution)/shard_map/ppermute | solution.py:294
  20.4 17.3 %collective-permute-start.2 = (bf16[1024,128]{1,0:T(8,128)(2,1)S(1)}, bf16[1024,128]{1,0:T(8,128)(2,1)S(1)}, u32[]{:S(2)}, u32[]{:S(2)}) collective-permute-start(bf16[1024,128]{1,0:T(8,128)(2,1)S(1)} %get-tuple-element.49), channel_id=1, source_target_pairs={{0,2},{1,3},{2,4},{3,5},{4,6},{5,7},{6,0},{7,1},{8,10},{9,11},{10,... | collective-permute-start | bytes 786440 | tf_op jit(solution)/shard_map/ppermute | solution.py:294
  21.0 16.6 %collective-permute-start.3 = (bf16[1024,128]{1,0:T(8,128)(2,1)S(1)}, bf16[1024,128]{1,0:T(8,128)(2,1)S(1)}, u32[]{:S(2)}, u32[]{:S(2)}) collective-permute-start(bf16[1024,128]{1,0:T(8,128)(2,1)S(1)} %get-tuple-element.50), channel_id=1, source_target_pairs={{0,6},{1,7},{2,0},{3,1},{4,2},{5,3},{6,4},{7,5},{8,14},{9,15},{10,... | collective-permute-start | bytes 786440 | tf_op jit(solution)/shard_map/ppermute | solution.py:294
  27.9 9.8 %copy-start.3 = (s32[512,1]{0,1:T(1,128)S(1)}, s32[512,1]{0,1:T(1,128)}, u32[]{:S(2)}) copy-start(s32[512,1]{0,1:T(1,128)} %param.8) | copy-start | bytes 6148
  27.9 9.8 %copy-start.4 = (s32[512]{0:T(512)S(1)}, s32[512]{0:T(512)}, u32[]{:S(2)}) copy-start(s32[512]{0:T(512)} %lengths_ref.7) | copy-start | bytes 6148
  27.9 20.8 %collective-permute-start.5 = (bf16[1024,128]{1,0:T(8,128)(2,1)}, bf16[1024,128]{1,0:T(8,128)(2,1)}, u32[]{:S(2)}, u32[]{:S(2)}) collective-permute-start(bf16[1024,128]{1,0:T(8,128)(2,1)} %get-tuple-element.56), channel_id=1, source_target_pairs={{0,4},{1,5},{2,6},{3,7},{4,0},{5,1},{6,2},{7,3},{8,12},{9,13},{10,... | collective-permute-start | bytes 786440 | tf_op jit(solution)/shard_map/ppermute | solution.py:294
  31.1 21.0 %collective-permute-start.6 = (bf16[1024,128]{1,0:T(8,128)(2,1)S(1)}, bf16[1024,128]{1,0:T(8,128)(2,1)}, u32[]{:S(2)}, u32[]{:S(2)}) collective-permute-start(bf16[1024,128]{1,0:T(8,128)(2,1)S(1)} %get-tuple-element.58), channel_id=1, source_target_pairs={{0,2},{1,3},{2,4},{3,5},{4,6},{5,7},{6,0},{7,1},{8,10},{9,11},{10,... | collective-permute-start | bytes 786440 | tf_op jit(solution)/shard_map/ppermute | solution.py:294
  31.8 20.3 %collective-permute-start.7 = (bf16[1024,128]{1,0:T(8,128)(2,1)S(1)}, bf16[1024,128]{1,0:T(8,128)(2,1)}, u32[]{:S(2)}, u32[]{:S(2)}) collective-permute-start(bf16[1024,128]{1,0:T(8,128)(2,1)S(1)} %get-tuple-element.59), channel_id=1, source_target_pairs={{0,6},{1,7},{2,0},{3,1},{4,2},{5,3},{6,4},{7,5},{8,14},{9,15},{10,... | collective-permute-start | bytes 786440 | tf_op jit(solution)/shard_map/ppermute | solution.py:294
  39.4 24.4 %all-to-all-start = ((bf16[32,64,128]{2,1,0:T(8,128)(2,1)}), bf16[32,64,128]{2,1,0:T(8,128)(2,1)S(1)}, u32[]{:S(2)}, u32[]{:S(2)}) async-start(bf16[32,64,128]{2,1,0:T(8,128)(2,1)} %shard_map.79), calls=%async_computation | async-start | bytes 1048576 | tf_op jit(solution)/shard_map/all_to_all | solution.py:317
  48.6 18.8 %collective-permute-start.8 = (bf16[2048,128]{1,0:T(8,128)(2,1)S(1)}, bf16[2048,128]{1,0:T(8,128)(2,1)}, u32[]{:S(2)}, u32[]{:S(2)}) collective-permute-start(bf16[2048,128]{1,0:T(8,128)(2,1)S(1)} %get-tuple-element.62), channel_id=1, source_target_pairs={{0,4},{1,5},{2,6},{3,7},{4,0},{5,1},{6,2},{7,3},{8,12},{9,13},{10,... | collective-permute-start | bytes 1572872 | tf_op jit(solution)/shard_map/ppermute | solution.py:294
  48.7 23.9 %collective-permute-start.9 = (bf16[2048,128]{1,0:T(8,128)(2,1)S(1)}, bf16[2048,128]{1,0:T(8,128)(2,1)}, u32[]{:S(2)}, u32[]{:S(2)}) collective-permute-start(bf16[2048,128]{1,0:T(8,128)(2,1)S(1)} %get-tuple-element.63), channel_id=1, source_target_pairs={{0,2},{1,3},{2,4},{3,5},{4,6},{5,7},{6,0},{7,1},{8,10},{9,11},{10,... | collective-permute-start | bytes 1572872 | tf_op jit(solution)/shard_map/ppermute | solution.py:294
  49.6 23.1 %collective-permute-start.10 = (bf16[2048,128]{1,0:T(8,128)(2,1)S(1)}, bf16[2048,128]{1,0:T(8,128)(2,1)}, u32[]{:S(2)}, u32[]{:S(2)}) collective-permute-start(bf16[2048,128]{1,0:T(8,128)(2,1)S(1)} %get-tuple-element.64), channel_id=1, source_target_pairs={{0,6},{1,7},{2,0},{3,1},{4,2},{5,3},{6,4},{7,5},{8,14},{9,15},{10,... | collective-permute-start | bytes 1572872 | tf_op jit(solution)/shard_map/ppermute | solution.py:294
  63.8 25.9 %all-to-all-start.1 = ((bf16[32,64,128]{2,1,0:T(8,128)(2,1)}), bf16[32,64,128]{2,1,0:T(8,128)(2,1)S(1)}, u32[]{:S(2)}, u32[]{:S(2)}) async-start(bf16[32,64,128]{2,1,0:T(8,128)(2,1)} %shard_map.82), calls=%async_computation.1 | async-start | bytes 1048576 | tf_op jit(solution)/shard_map/all_to_all | solution.py:317
  67.4 18.0 %copy-start.5 = (bf16[1,1,16,2,4,1024]{5,4,3,2,1,0:T(4,128)(2,1)S(1)}, bf16[1,1,16,2,4,1024]{5,4,3,2,1,0:T(4,128)(2,1)}, u32[]{:S(2)}) copy-start(bf16[1,1,16,2,4,1024]{5,4,3,2,1,0:T(4,128)(2,1)} %param.10) | copy-start | bytes 786436
  67.4 22.4 %copy-start.2 = (bf16[1,1,16,2,4,256]{5,4,3,2,1,0:T(4,128)(2,1)S(1)}, bf16[1,1,16,2,4,256]{5,4,3,2,1,0:T(4,128)(2,1)}, u32[]{:S(2)}) copy-start(bf16[1,1,16,2,4,256]{5,4,3,2,1,0:T(4,128)(2,1)} %param.11) | copy-start | bytes 196612
  74.8 18.5 %collective-permute-start.11 = (bf16[2,2,128,128]{3,2,1,0:T(8,128)(2,1)S(1)}, bf16[2,2,128,128]{3,2,1,0:T(8,128)(2,1)S(1)}, u32[]{:S(2)}, u32[]{:S(2)}) collective-permute-start(bf16[2,2,128,128]{3,2,1,0:T(8,128)(2,1)S(1)} %get-tuple-element.65), channel_id=1, source_target_pairs={{0,128},{16,144},{32,160},{48,176},{64,192},{80,208},{96,224},{112... | collective-permute-start | bytes 393224 | tf_op jit(solution)/shard_map/ppermute | solution.py:328
  80.4 17.5 %collective-permute-start.15 = (bf16[2,2,128,128]{3,2,1,0:T(8,128)(2,1)S(1)}, bf16[2,2,128,128]{3,2,1,0:T(8,128)(2,1)S(1)}, u32[]{:S(2)}, u32[]{:S(2)}) collective-permute-start(bf16[2,2,128,128]{3,2,1,0:T(8,128)(2,1)S(1)} %get-tuple-element.73), channel_id=1, source_target_pairs={{0,96},{16,112},{32,128},{48,144},{64,160},{80,176},{96,192},{112,... | collective-permute-start | bytes 393224 | tf_op jit(solution)/shard_map/ppermute | solution.py:328
  81.0 17.1 %collective-permute-start.16 = (bf16[2,2,128,128]{3,2,1,0:T(8,128)(2,1)S(1)}, bf16[2,2,128,128]{3,2,1,0:T(8,128)(2,1)S(1)}, u32[]{:S(2)}, u32[]{:S(2)}) collective-permute-start(bf16[2,2,128,128]{3,2,1,0:T(8,128)(2,1)S(1)} %get-tuple-element.75), channel_id=1, source_target_pairs={{0,160},{16,176},{32,192},{48,208},{64,224},{80,240},{96,0},{112,1... | collective-permute-start | bytes 393224 | tf_op jit(solution)/shard_map/ppermute | solution.py:328
  85.5 14.9 %collective-permute-start.14 = (bf16[2,2,128,128]{3,2,1,0:T(8,128)(2,1)S(1)}, bf16[2,2,128,128]{3,2,1,0:T(8,128)(2,1)S(1)}, u32[]{:S(2)}, u32[]{:S(2)}) collective-permute-start(bf16[2,2,128,128]{3,2,1,0:T(8,128)(2,1)S(1)} %get-tuple-element.72), channel_id=1, source_target_pairs={{0,64},{16,80},{32,96},{48,112},{64,128},{80,144},{96,160},{112,17... | collective-permute-start | bytes 393224 | tf_op jit(solution)/shard_map/ppermute | solution.py:328
  86.2 14.9 %collective-permute-start.17 = (bf16[2,2,128,128]{3,2,1,0:T(8,128)(2,1)S(1)}, bf16[2,2,128,128]{3,2,1,0:T(8,128)(2,1)S(1)}, u32[]{:S(2)}, u32[]{:S(2)}) collective-permute-start(bf16[2,2,128,128]{3,2,1,0:T(8,128)(2,1)S(1)} %get-tuple-element.76), channel_id=1, source_target_pairs={{0,192},{16,208},{32,224},{48,240},{64,0},{80,16},{96,32},{112,48}... | collective-permute-start | bytes 393224 | tf_op jit(solution)/shard_map/ppermute | solution.py:328
  98.1 13.8 %collective-permute-start.20 = (bf16[4,2,128,128]{3,2,1,0:T(8,128)(2,1)S(1)}, bf16[4,2,128,128]{3,2,1,0:T(8,128)(2,1)S(1)}, u32[]{:S(2)}, u32[]{:S(2)}) collective-permute-start(bf16[4,2,128,128]{3,2,1,0:T(8,128)(2,1)S(1)} %shard_map.85), channel_id=1, source_target_pairs={{0,16},{16,0},{32,48},{48,32},{64,80},{80,64},{96,112},{112,96},{1... | collective-permute-start | bytes 786440 | tf_op jit(solution)/shard_map/ppermute | solution.py:363
  99.7 6.2 %collective-permute-start.12 = (bf16[2,128,128]{2,1,0:T(8,128)(2,1)S(1)}, bf16[2,128,128]{2,1,0:T(8,128)(2,1)S(1)}, u32[]{:S(2)}, u32[]{:S(2)}) collective-permute-start(bf16[2,128,128]{2,1,0:T(8,128)(2,1)S(1)} %get-tuple-element.70), channel_id=1, source_target_pairs={{0,32},{16,48},{32,64},{48,80},{64,96},{80,112},{96,128},{112,144}... | collective-permute-start | bytes 196616 | tf_op jit(solution)/shard_map/ppermute | solution.py:330
  101.1 10.8 %collective-permute-start.21 = (bf16[2,2,128,128]{3,2,1,0:T(8,128)(2,1)S(1)}, bf16[2,2,128,128]{3,2,1,0:T(8,128)(2,1)S(1)}, u32[]{:S(2)}, u32[]{:S(2)}) collective-permute-start(bf16[2,2,128,128]{3,2,1,0:T(8,128)(2,1)S(1)} %shard_map.86), channel_id=1, source_target_pairs={{0,16},{16,0},{32,48},{48,32},{64,80},{80,64},{96,112},{112,96},{1... | collective-permute-start | bytes 393224 | tf_op jit(solution)/shard_map/ppermute | solution.py:363
  102.6 6.7 %collective-permute-start.13 = (bf16[2,128,128]{2,1,0:T(8,128)(2,1)S(1)}, bf16[2,128,128]{2,1,0:T(8,128)(2,1)S(1)}, u32[]{:S(2)}, u32[]{:S(2)}) collective-permute-start(bf16[2,128,128]{2,1,0:T(8,128)(2,1)S(1)} %get-tuple-element.71), channel_id=1, source_target_pairs={{0,48},{16,32},{32,80},{48,64},{64,112},{80,96},{96,144},{112,128}... | collective-permute-start | bytes 196616 | tf_op jit(solution)/shard_map/ppermute | solution.py:330
  104.1 5.2 %collective-permute-start.18 = (bf16[2,128,128]{2,1,0:T(8,128)(2,1)S(1)}, bf16[2,128,128]{2,1,0:T(8,128)(2,1)S(1)}, u32[]{:S(2)}, u32[]{:S(2)}) collective-permute-start(bf16[2,128,128]{2,1,0:T(8,128)(2,1)S(1)} %get-tuple-element.77), channel_id=1, source_target_pairs={{0,224},{16,240},{32,0},{48,16},{64,32},{80,48},{96,64},{112,80},{... | collective-permute-start | bytes 196616 | tf_op jit(solution)/shard_map/ppermute | solution.py:330
  105.9 5.2 %collective-permute-start.19 = (bf16[2,128,128]{2,1,0:T(8,128)(2,1)S(1)}, bf16[2,128,128]{2,1,0:T(8,128)(2,1)S(1)}, u32[]{:S(2)}, u32[]{:S(2)}) collective-permute-start(bf16[2,128,128]{2,1,0:T(8,128)(2,1)S(1)} %get-tuple-element.78), channel_id=1, source_target_pairs={{0,240},{16,224},{32,16},{48,0},{64,48},{80,32},{96,80},{112,64},{... | collective-permute-start | bytes 196616 | tf_op jit(solution)/shard_map/ppermute | solution.py:330

commit v2 on v1

--- a/solution.py
+++ b/solution.py
@@ -11,7 +11,7 @@
 KV_HEADS = 8
 HD = 128
 CAP = 2
-TILE = 256
+TILE = 512
 DIRECT = (1, 7)
 FAR_FIRST = (4, 3, 5, 2, 6)
 FORWARD = ((0, 4, 3, 5), (2, 6))
@@ -166,7 +166,7 @@
     fresh_ids = lax.broadcasted_iota(jnp.int32, (many, batch * steps), 1)
     seen = jnp.logical_and(
         row_ids // rows == fresh_ids // steps,
-        fresh_ids % steps <= row_ids % rows // (rows // steps),
+        fresh_ids % steps <= row_ids % steps,
     )
     for start in range(0, slots, batch):
         group = slice(start, start + batch)
@@ -220,7 +220,10 @@
                 weight_ref[slot], vals_ref[c], CONTRACT_LAST, preferred_element_type=jnp.float32
             )
             mixed = summed * scale_ref[slot] + fresh_out_ref[slot]
-            out_ref[slot] = mixed.astype(jnp.bfloat16)
+            steps = out_ref.shape[1]
+            for h in range(mixed.shape[0] // steps):
+                block = mixed[h * steps : (h + 1) * steps].astype(jnp.bfloat16)
+                out_ref[slot, :, h * HD : (h + 1) * HD] = block
     for copy in copies:
         copy.wait()
 
@@ -286,12 +289,13 @@
             else [shaped(token_count, HD)] * ys,
         )(info, flat_tokens, kv_weight, came[0 if split else 1])
         sums += [made[:ys], made[ys:]] if split else [made]
+    sums[1], sums[2] = lax.optimization_barrier((sums[1], sums[2]))
     summed = []
     for part in sums:
         if summed:
             part, summed[-1][1] = lax.optimization_barrier((part, summed[-1][1]))
         summed.append(
-            [part[0]] + [lax.ppermute(part[d], "tensor", y_pairs[d]) for d in (2, 1, 3)]
+            [part[0]] + [lax.ppermute(part[d], "tensor", y_pairs[d]) for d in (1, 3, 2)]
         )
 
     def place(part, relative, out_shape):
@@ -346,7 +350,9 @@
         info,
         flat_routes,
         lengths,
-        queries.reshape(slots, rows, HD),
+        jnp.swapaxes(queries.reshape(slots, step_count, per_group, HD), 1, 2).reshape(
+            slots, rows, HD
+        ),
         new_kv.reshape(slots, step_count, 2 * HD),
         *keys,
     )
@@ -370,7 +376,10 @@
         functools.partial(mix_kernel, zs),
         in_specs=smem_specs(1) + vmem_specs(3 + len(vals)) + any_specs(1),
         out_specs=any_specs(1) + vmem_specs(1),
-        out_shape=[shaped(slots, col_here, positions), shaped(slots, rows, HD)],
+        out_shape=[
+            shaped(slots, col_here, positions),
+            shaped(slots, step_count, per_group * HD),
+        ],
         scratch_shapes=[pltpu.SemaphoreType.DMA((groups,))],
         input_output_aliases={4 + len(vals): 0},
     )(info, weights, scales, fresh_out, *vals, cache)

time: 115 us -> 112 us (0.974)
  waiting for transfers between devices: 29.7 us -> 26.2 us
    ppermute x9, waiting for transfers between devices: 9.53 us -> 5.91 us  [per_device(): lax.ppermute(part[d], 'tensor', y_pairs[d])]
    ppermute x4, starting transfers between devices: 5.16 us -> 7.59 us  [per_device(): lax.ppermute(pieces[d][e], 'group', z_pairs[d, e])]
    ppermute x2, starting transfers between devices: 3.1 us -> 1.09 us  [per_device(): passed.append(lax.ppermute(halves, 'group', z_pairs[0, 1]))]
    ppermute x9, starting transfers between devices: 16.3 us -> 17.5 us  [per_device(): lax.ppermute(part[d], 'tensor', y_pairs[d])]
    unnamed x12 -> x16, local copies, waits for them, and re-layouts: 4.4 us -> 5.03 us
  transfers between devices with their start and end apart: 24 -> 24, of which waited for: 10 -> 7; matrix products, arithmetic and copies ran while one was open for 0% -> 0% of each run, Pallas kernels for 18% -> 18%
where the time goes in v2:
time: 112 us
  starting transfers between devices  53.4 us (48%)
  waiting for transfers between devices  26.2 us (23%)
  Pallas kernels  26 us (23%)
  local copies, waits for them, and re-layouts  5.11 us (5%)
    ppermute x9, starting transfers between devices, per_device(): lax.ppermute(part[d], 'tensor', y_pairs[d])  17.5 us
    ppermute x5, starting transfers between devices, per_device(): pieces[d] = lax.ppermute(pieces[d], 'group', z_pairs[d, 0])  14.7 us
    all_to_all x2, starting transfers between devices, per_device(): keys.append(lax.all_to_all(placed, 'group', 0, 0, tiled=True))  11.9 us
    all_to_all x2, waiting for transfers between devices, per_device(): keys.append(lax.all_to_all(placed, 'group', 0, 0, tiled=True))  10.1 us
    ppermute x4, starting transfers between devices, per_device(): lax.ppermute(pieces[d][e], 'group', z_pairs[d, e])  7.59 us
    pallas_call x2, Pallas kernels, per_device(): call(functools.partial(project_kernel, split, True), in_specs=smem_specs(...  7.34 us
    pallas_call x2, Pallas kernels, per_device(): call(functools.partial(project_kernel, split, False), in_specs=smem_specs...  6.25 us
    pallas_call x3, Pallas kernels, place(): call(functools.partial(place_kernel, relative), in_specs=smem_specs(3) +...  5.96 us
  transfers between devices with their start and end apart: 24, of which 7 were waited for; matrix products, arithmetic and copies ran while one was open for 0% of the time, Pallas kernels for 18%

profile of v2, /device:TPU:4, one launch (start us, length us, event | category | flops | bytes accessed | tf_op | source)
XLA Modules:
  0.0 111.7 jit_solution(17205234209610058111)
XLA Ops:
  0.7 0.1 stack.23.info_ref
  0.7 2.2 %copy-done = bf16[16,128,1024]{2,1,0:T(8,128)(2,1)S(1)} copy-done((bf16[16,128,1024]{2,1,0:T(8,128)(2,1)S(1)}, bf16[16,128,1024]{2,1,0:T(8,128)(2,1)}, u32[]{:S(2)}) %copy-start) | copy-done | bytes 4194328
  2.9 2.2 %copy-done.1 = bf16[1024,2048]{1,0:T(8,128)(2,1)S(1)} copy-done((bf16[1024,2048]{1,0:T(8,128)(2,1)S(1)}, bf16[1024,2048]{1,0:T(8,128)(2,1)}, u32[]{:S(2)}) %copy-start.1) | copy-done | bytes 4194328
  5.1 3.2 %shard_map.77 = bf16[8,1024,128]{2,1,0:T(8,128)(2,1)S(1)} custom-call(s32[6]{0:T(128)S(1)} %stack.23.info_ref, bf16[2048,1024]{1,0:T(8,128)(2,1)S(1)} %bitcast.15, bf16[1024,2048]{1,0:T(8,128)(2,1)S(1)} %copy-done.1), custom_call_target="tpu_custom_call" | custom-call | tf_op jit(solution)/shard_map/pallas_call | solution.py:274
  8.4 0.1 collective-permute-start
  8.5 3.0 %shard_map.79 = bf16[4,2048,128]{2,1,0:T(8,128)(2,1)S(1)} custom-call(s32[6]{0:T(128)S(1)} %stack.23.info_ref, bf16[2048,1024]{1,0:T(8,128)(2,1)S(1)} %bitcast.16, bf16[1024,2048]{1,0:T(8,128)(2,1)S(1)} %copy-done.1), custom_call_target="tpu_custom_call" | custom-call | tf_op jit(solution)/shard_map/pallas_call | solution.py:274
  11.5 0.5 collective-permute-start.1
  12.0 0.6 collective-permute-done.refs_0_
  12.6 3.5 %shard_map.78 = (bf16[1024,128]{1,0:T(8,128)(2,1)S(1)}, bf16[1024,128]{1,0:T(8,128)(2,1)S(1)}, bf16[1024,128]{1,0:T(8,128)(2,1)S(1)}, bf16[1024,128]{1,0:T(8,128...) custom-call(s32[6]{0:T(128)S(1)} %stack.23.info_ref, ...), custom_call_target="tpu_custom_call" | custom-call | tf_op jit(solution)/shard_map/pallas_call | solution.py:283
  16.1 1.7 %collective-permute-start.2 = (bf16[1024,128]{1,0:T(8,128)(2,1)S(1)}, bf16[1024,128]{1,0:T(8,128)(2,1)S(1)}, u32[]{:S(2)}, u32[]{:S(2)}) collective-permute-start(bf16[1024,128]{1,0:T(8,128)(2,1)S(1)} %get-tuple-element.63), channel_id=1, source_target_pairs={{0,2},{1,3},{2,4},{3,5},{4,6},{5,7},{6,0},{7,1},{8,10},{9,11},{10,... | collective-permute-start | bytes 786440 | tf_op jit(solution)/shard_map/ppermute | solution.py:298
  17.8 1.7 %collective-permute-start.3 = (bf16[1024,128]{1,0:T(8,128)(2,1)S(1)}, bf16[1024,128]{1,0:T(8,128)(2,1)S(1)}, u32[]{:S(2)}, u32[]{:S(2)}) collective-permute-start(bf16[1024,128]{1,0:T(8,128)(2,1)S(1)} %get-tuple-element.65), channel_id=1, source_target_pairs={{0,6},{1,7},{2,0},{3,1},{4,2},{5,3},{6,4},{7,5},{8,14},{9,15},{10,... | collective-permute-start | bytes 786440 | tf_op jit(solution)/shard_map/ppermute | solution.py:298
  19.4 2.0 %collective-permute-start.4 = (bf16[1024,128]{1,0:T(8,128)(2,1)S(1)}, bf16[1024,128]{1,0:T(8,128)(2,1)S(1)}, u32[]{:S(2)}, u32[]{:S(2)}) collective-permute-start(bf16[1024,128]{1,0:T(8,128)(2,1)S(1)} %get-tuple-element.66), channel_id=1, source_target_pairs={{0,4},{1,5},{2,6},{3,7},{4,0},{5,1},{6,2},{7,3},{8,12},{9,13},{10,... | collective-permute-start | bytes 786440 | tf_op jit(solution)/shard_map/ppermute | solution.py:298
  21.4 0.0 collective-permute-done.1.refs_0_
  21.4 3.8 %shard_map.80 = (bf16[2048,128]{1,0:T(8,128)(2,1)S(1)}, bf16[2048,128]{1,0:T(8,128)(2,1)}, bf16[2048,128]{1,0:T(8,128)(2,1)S(1)}, bf16[2048,128]{1,0:T(8,128)(2,1)S(1)}) custom-call(s32[6]{0:T(128)S(1)} %stack.23.info_ref, bf16[2048,1024]{1,0:T(8,128)(2,1)S(1)} %bitcast.18, bf16[1024,2048]{1,0:T(8,128)(2,1)S(1)} %copy-done.1, ...), custom_call_target="tpu_custom_call" | custom-call | tf_op jit(solution)/shard_map/pallas_call | solution.py:283
  25.2 0.6 collective-permute-done.2.refs_1_
  25.8 1.1 collective-permute-start.5
  26.9 2.1 %collective-permute-start.6 = (bf16[1024,128]{1,0:T(8,128)(2,1)S(1)}, bf16[1024,128]{1,0:T(8,128)(2,1)}, u32[]{:S(2)}, u32[]{:S(2)}) collective-permute-start(bf16[1024,128]{1,0:T(8,128)(2,1)S(1)} %get-tuple-element.74), channel_id=1, source_target_pairs={{0,6},{1,7},{2,0},{3,1},{4,2},{5,3},{6,4},{7,5},{8,14},{9,15},{10,... | collective-permute-start | bytes 786440 | tf_op jit(solution)/shard_map/ppermute | solution.py:298
  29.0 5.6 %collective-permute-start.7 = (bf16[1024,128]{1,0:T(8,128)(2,1)S(1)}, bf16[1024,128]{1,0:T(8,128)(2,1)}, u32[]{:S(2)}, u32[]{:S(2)}) collective-permute-start(bf16[1024,128]{1,0:T(8,128)(2,1)S(1)} %get-tuple-element.75), channel_id=1, source_target_pairs={{0,4},{1,5},{2,6},{3,7},{4,0},{5,1},{6,2},{7,3},{8,12},{9,13},{10,... | collective-permute-start | bytes 786440 | tf_op jit(solution)/shard_map/ppermute | solution.py:298
  34.6 0.0 collective-permute-done.3.refs_2_
  34.6 0.0 collective-permute-done.4.refs_3_
  34.6 1.7 %shard_map.81 = bf16[32,64,128]{2,1,0:T(8,128)(2,1)} custom-call(s32[6]{0:T(128)S(1)} %stack.23.info_ref, s32[512]{0:T(512)S(1)} %bitcast.21, s32[512]{0:T(512)S(1)} %copy-done.5, bf16[1024,128]{1,0:T(8,128)(2,1)S(1)} %get-tuple-element.50.refs_0_, bf16[1024,128]{1,0:T(8,128)(2,1)S(1)} %collective-permute-done.2.refs_1_, ...), custom_call_target="tpu_custom_call" | custom-call | tf_op jit(solution)/shard_map/pallas_call | solution.py:302
  36.4 8.3 %all-to-all-start = ((bf16[32,64,128]{2,1,0:T(8,128)(2,1)}), bf16[32,64,128]{2,1,0:T(8,128)(2,1)S(1)}, u32[]{:S(2)}, u32[]{:S(2)}) async-start(bf16[32,64,128]{2,1,0:T(8,128)(2,1)} %shard_map.81), calls=%async_computation | async-start | bytes 1048576 | tf_op jit(solution)/shard_map/all_to_all | solution.py:321
  44.7 0.0 collective-permute-done.5.refs_1_
  44.7 1.2 %collective-permute-start.8 = (bf16[2048,128]{1,0:T(8,128)(2,1)}, bf16[2048,128]{1,0:T(8,128)(2,1)}, u32[]{:S(2)}, u32[]{:S(2)}) collective-permute-start(bf16[2048,128]{1,0:T(8,128)(2,1)} %get-tuple-element.78), channel_id=1, source_target_pairs={{0,2},{1,3},{2,4},{3,5},{4,6},{5,7},{6,0},{7,1},{8,10},{9,11},{10,... | collective-permute-start | bytes 1572872 | tf_op jit(solution)/shard_map/ppermute | solution.py:298
  45.9 2.1 %collective-permute-start.9 = (bf16[2048,128]{1,0:T(8,128)(2,1)S(1)}, bf16[2048,128]{1,0:T(8,128)(2,1)}, u32[]{:S(2)}, u32[]{:S(2)}) collective-permute-start(bf16[2048,128]{1,0:T(8,128)(2,1)S(1)} %get-tuple-element.79), channel_id=1, source_target_pairs={{0,6},{1,7},{2,0},{3,1},{4,2},{5,3},{6,4},{7,5},{8,14},{9,15},{10,... | collective-permute-start | bytes 1572872 | tf_op jit(solution)/shard_map/ppermute | solution.py:298
  48.0 0.1 collective-permute-start.10
  48.1 0.0 collective-permute-done.6.refs_2_
  48.1 0.0 collective-permute-done.7.refs_3_
  48.1 2.2 %shard_map.82 = bf16[32,64,128]{2,1,0:T(8,128)(2,1)} custom-call(s32[6]{0:T(128)S(1)} %stack.23.info_ref, s32[512]{0:T(512)S(1)} %bitcast.22, s32[512]{0:T(512)S(1)} %copy-done.5, bf16[1024,128]{1,0:T(8,128)(2,1)S(1)} %get-tuple-element.67.refs_0_, bf16[1024,128]{1,0:T(8,128)(2,1)S(1)} %collective-permute-done.5.refs_1_, ...), custom_call_target="tpu_custom_call" | custom-call | flops 30000001024 | tf_op jit(solution)/shard_map/pallas_call | solution.py:302
  50.3 10.1 %all-to-all-done.refs_0_ = bf16[32,64,128]{2,1,0:T(8,128)(2,1)S(1)} async-done(((bf16[32,64,128]{2,1,0:T(8,128)(2,1)}), bf16[32,64,128]{2,1,0:T(8,128)(2,1)S(1)}, u32[]{:S(2)}, u32[]{:S(2)}) %all-to-all-start) | async-done | bytes 524320 | tf_op jit(solution)/shard_map/all_to_all | solution.py:321
  60.3 3.6 %all-to-all-start.1 = ((bf16[32,64,128]{2,1,0:T(8,128)(2,1)}), bf16[32,64,128]{2,1,0:T(8,128)(2,1)S(1)}, u32[]{:S(2)}, u32[]{:S(2)}) async-start(bf16[32,64,128]{2,1,0:T(8,128)(2,1)} %shard_map.82), calls=%async_computation.1 | async-start | bytes 1048576 | tf_op jit(solution)/shard_map/all_to_all | solution.py:321
  63.9 0.0 copy-start.2
  63.9 0.0 copy-start.3
  64.0 5.3 %collective-permute-done.8.refs_1_ = bf16[2048,128]{1,0:T(8,128)(2,1)} collective-permute-done((bf16[2048,128]{1,0:T(8,128)(2,1)}, bf16[2048,128]{1,0:T(8,128)(2,1)}, u32[]{:S(2)}, u32[]{:S(2)}) %collective-permute-start.8) | collective-permute-done | bytes 524320 | tf_op jit(solution)/shard_map/ppermute | solution.py:298
  69.3 0.0 collective-permute-done.9.refs_2_
  69.3 0.0 collective-permute-done.10.refs_3_
  69.3 2.1 %shard_map.84 = (bf16[2,2,128,128]{3,2,1,0:T(8,128)(2,1)S(1)}, bf16[2,128,128]{2,1,0:T(8,128)(2,1)S(1)}, bf16[2,128,128]{2,1,0:T(8,128)(2,1)S(1)}, bf16[2,2,128,...) custom-call(s32[6]{0:T(128)S(1)} %stack.23.info_ref, ...), custom_call_target="tpu_custom_call" | custom-call | flops 30000001024 | tf_op jit(solution)/shard_map/pallas_call | solution.py:302
  71.4 0.0 copy-start.6
  71.4 0.6 copy-done.6
  72.0 5.6 %collective-permute-start.11 = (bf16[2,2,128,128]{3,2,1,0:T(8,128)(2,1)S(1)}, bf16[2,2,128,128]{3,2,1,0:T(8,128)(2,1)S(1)}, u32[]{:S(2)}, u32[]{:S(2)}) collective-permute-start(bf16[2,2,128,128]{3,2,1,0:T(8,128)(2,1)S(1)} %get-tuple-element.81), channel_id=1, source_target_pairs={{0,128},{16,144},{32,160},{48,176},{64,192},{80,208},{96,224},{112... | collective-permute-start | bytes 393224 | tf_op jit(solution)/shard_map/ppermute | solution.py:332
  77.6 1.0 collective-permute-start.15
  78.6 4.1 %collective-permute-start.16 = (bf16[2,2,128,128]{3,2,1,0:T(8,128)(2,1)S(1)}, bf16[2,2,128,128]{3,2,1,0:T(8,128)(2,1)S(1)}, u32[]{:S(2)}, u32[]{:S(2)}) collective-permute-start(bf16[2,2,128,128]{3,2,1,0:T(8,128)(2,1)S(1)} %get-tuple-element.91), channel_id=1, source_target_pairs={{0,160},{16,176},{32,192},{48,208},{64,224},{80,240},{96,0},{112,1... | collective-permute-start | bytes 393224 | tf_op jit(solution)/shard_map/ppermute | solution.py:332
  82.6 0.6 collective-permute-start.14
  83.2 3.6 %collective-permute-start.17 = (bf16[2,2,128,128]{3,2,1,0:T(8,128)(2,1)S(1)}, bf16[2,2,128,128]{3,2,1,0:T(8,128)(2,1)S(1)}, u32[]{:S(2)}, u32[]{:S(2)}) collective-permute-start(bf16[2,2,128,128]{3,2,1,0:T(8,128)(2,1)S(1)} %get-tuple-element.92), channel_id=1, source_target_pairs={{0,192},{16,208},{32,224},{48,240},{64,0},{80,16},{96,32},{112,48}... | collective-permute-start | bytes 393224 | tf_op jit(solution)/shard_map/ppermute | solution.py:332
  86.7 0.0 all-to-all-done.1.refs_1_
  86.8 3.5 %shard_map.83 = (bf16[32,256,128]{2,1,0:T(8,128)(2,1)}, bf16[32,32,128]{2,1,0:T(8,128)(2,1)S(1)}, f32[32,32,128]{2,1,0:T(8,128)S(1)}, f32[32,32,128]{2,1,0:T(8,128)S(1)}) custom-call(s32[6]{0:T(128)S(1)} %stack.23.info_ref, s32[512]{0:T(512)S(1)} %bitcast.24, s32[512]{0:T(512)S(1)} %copy-done.5, bf16[32,32,128]{2,1,0:T(8,128)(2,1)S(1)} %bitcast.19, ...), custom_call_target="tpu_custom_call" | custom-call | tf_op jit(solution)/shard_map/pallas_call | solution.py:335
  90.3 0.0 collective-permute-done.11.refs_1_.refs_5_
  90.3 4.5 %collective-permute-done.15.refs_2_.refs_4_ = bf16[2,2,128,128]{3,2,1,0:T(8,128)(2,1)S(1)} collective-permute-done((bf16[2,2,128,128]{3,2,1,0:T(8,128)(2,1)S(1)}, bf16[2,2,128,128]{3,2,1,0:T(8,128)(2,1)S(1)}, u32[]{:S(2)}, u32[]{:S(2)}) %collective-permute-start.15) | collective-permute-done | bytes 131104 | tf_op jit(solution)/shard_map/ppermute | solution.py:332
  94.8 0.0 collective-permute-done.16.refs_3_.refs_6_
  94.8 0.9 collective-permute-start.20
  95.7 3.0 %collective-permute-start.12 = (bf16[2,128,128]{2,1,0:T(8,128)(2,1)S(1)}, bf16[2,128,128]{2,1,0:T(8,128)(2,1)S(1)}, u32[]{:S(2)}, u32[]{:S(2)}) collective-permute-start(bf16[2,128,128]{2,1,0:T(8,128)(2,1)S(1)} %copy-done.7), channel_id=1, source_target_pairs={{0,32},{16,48},{32,64},{48,80},{64,96},{80,112},{96,128},{112,144}... | collective-permute-start | bytes 196616 | tf_op jit(solution)/shard_map/ppermute | solution.py:334
  98.7 0.0 collective-permute-done.14.refs_0_.refs_3_
  98.7 0.0 collective-permute-done.17.refs_1_.refs_7_
  98.7 0.2 collective-permute-start.21
  98.9 1.7 %collective-permute-start.13 = (bf16[2,128,128]{2,1,0:T(8,128)(2,1)S(1)}, bf16[2,128,128]{2,1,0:T(8,128)(2,1)S(1)}, u32[]{:S(2)}, u32[]{:S(2)}) collective-permute-start(bf16[2,128,128]{2,1,0:T(8,128)(2,1)S(1)} %get-tuple-element.87), channel_id=1, source_target_pairs={{0,48},{16,32},{32,80},{48,64},{64,112},{80,96},{96,144},{112,128}... | collective-permute-start | bytes 196616 | tf_op jit(solution)/shard_map/ppermute | solution.py:334
  100.5 2.9 %collective-permute-start.18 = (bf16[2,128,128]{2,1,0:T(8,128)(2,1)S(1)}, bf16[2,128,128]{2,1,0:T(8,128)(2,1)S(1)}, u32[]{:S(2)}, u32[]{:S(2)}) collective-permute-start(bf16[2,128,128]{2,1,0:T(8,128)(2,1)S(1)} %get-tuple-element.93), channel_id=1, source_target_pairs={{0,224},{16,240},{32,0},{48,16},{64,32},{80,48},{96,64},{112,80},{... | collective-permute-start | bytes 196616 | tf_op jit(solution)/shard_map/ppermute | solution.py:334
  103.5 0.0 collective-permute-done.12.refs_1_
  103.5 0.0 collective-permute-start.19
  103.5 1.9 %collective-permute-done.13.refs_2_ = bf16[2,128,128]{2,1,0:T(8,128)(2,1)S(1)} collective-permute-done((bf16[2,128,128]{2,1,0:T(8,128)(2,1)S(1)}, bf16[2,128,128]{2,1,0:T(8,128)(2,1)S(1)}, u32[]{:S(2)}, u32[]{:S(2)}) %collective-permute-start.13) | collective-permute-done | bytes 65568 | tf_op jit(solution)/shard_map/ppermute | solution.py:334
  105.4 0.0 collective-permute-done.18.refs_8_
  105.4 3.2 %collective-permute-done.19.refs_9_ = bf16[2,128,128]{2,1,0:T(8,128)(2,1)S(1)} collective-permute-done((bf16[2,128,128]{2,1,0:T(8,128)(2,1)S(1)}, bf16[2,128,128]{2,1,0:T(8,128)(2,1)S(1)}, u32[]{:S(2)}, u32[]{:S(2)}) %collective-permute-start.19) | collective-permute-done | bytes 65568 | tf_op jit(solution)/shard_map/ppermute | solution.py:334
  108.7 0.0 collective-permute-done.21.refs_11_
  108.7 0.0 collective-permute-done.20.refs_10_
  108.7 2.9 %shard_map.87 = (bf16[32,256,128]{2,1,0:T(8,128)(2,1)}, bf16[32,4,1024]{2,1,0:T(4,128)(2,1)}) custom-call(s32[6]{0:T(128)S(1)} %stack.23.info_ref, bf16[32,32,128]{2,1,0:T(8,128)(2,1)S(1)} %get-tuple-element.82.weight_ref, f32[32,32,128]{2,1,0:T(8,128)S(1)} %get-tuple-element.83.scale_ref, ...), custom_call_target="tpu_custom_call", output_to_operand_aliasing={{0}: (16, {})} | custom-call | tf_op jit(solution)/shard_map/pallas_call | solution.py:375
  (12 shorter events, 0.0 us)
Async XLA Ops:
  0.7 2.2 %copy-start = (bf16[16,128,1024]{2,1,0:T(8,128)(2,1)S(1)}, bf16[16,128,1024]{2,1,0:T(8,128)(2,1)}, u32[]{:S(2)}) copy-start(bf16[16,128,1024]{2,1,0:T(8,128)(2,1)} %param.6) | copy-start | bytes 12582916
  2.9 2.2 %copy-start.1 = (bf16[1024,2048]{1,0:T(8,128)(2,1)S(1)}, bf16[1024,2048]{1,0:T(8,128)(2,1)}, u32[]{:S(2)}) copy-start(bf16[1024,2048]{1,0:T(8,128)(2,1)} %weight_ref.7) | copy-start | bytes 12582916
  8.4 4.2 %collective-permute-start = (bf16[8,1024,128]{2,1,0:T(8,128)(2,1)S(1)}, bf16[8,1024,128]{2,1,0:T(8,128)(2,1)S(1)}, u32[]{:S(2)}, u32[]{:S(2)}) collective-permute-start(bf16[8,1024,128]{2,1,0:T(8,128)(2,1)S(1)} %shard_map.77), channel_id=1, source_target_pairs={{0,1},{1,0},{2,3},{3,2},{4,5},{5,4},{6,7},{7,6},{8,9},{9,8},{10,11... | collective-permute-start | bytes 6291464 | tf_op jit(solution)/shard_map/ppermute | solution.py:280
  11.5 9.9 %collective-permute-start.1 = (bf16[4,2048,128]{2,1,0:T(8,128)(2,1)S(1)}, bf16[4,2048,128]{2,1,0:T(8,128)(2,1)S(1)}, u32[]{:S(2)}, u32[]{:S(2)}) collective-permute-start(bf16[4,2048,128]{2,1,0:T(8,128)(2,1)S(1)} %shard_map.79), channel_id=1, source_target_pairs={{0,1},{1,0},{2,3},{3,2},{4,5},{5,4},{6,7},{7,6},{8,9},{9,8},{10,11... | collective-permute-start | bytes 6291464 | tf_op jit(solution)/shard_map/ppermute | solution.py:280
  16.1 9.7 %collective-permute-start.2 = (bf16[1024,128]{1,0:T(8,128)(2,1)S(1)}, bf16[1024,128]{1,0:T(8,128)(2,1)S(1)}, u32[]{:S(2)}, u32[]{:S(2)}) collective-permute-start(bf16[1024,128]{1,0:T(8,128)(2,1)S(1)} %get-tuple-element.63), channel_id=1, source_target_pairs={{0,2},{1,3},{2,4},{3,5},{4,6},{5,7},{6,0},{7,1},{8,10},{9,11},{10,... | collective-permute-start | bytes 786440 | tf_op jit(solution)/shard_map/ppermute | solution.py:298
  17.8 16.9 %collective-permute-start.3 = (bf16[1024,128]{1,0:T(8,128)(2,1)S(1)}, bf16[1024,128]{1,0:T(8,128)(2,1)S(1)}, u32[]{:S(2)}, u32[]{:S(2)}) collective-permute-start(bf16[1024,128]{1,0:T(8,128)(2,1)S(1)} %get-tuple-element.65), channel_id=1, source_target_pairs={{0,6},{1,7},{2,0},{3,1},{4,2},{5,3},{6,4},{7,5},{8,14},{9,15},{10,... | collective-permute-start | bytes 786440 | tf_op jit(solution)/shard_map/ppermute | solution.py:298
  19.4 15.2 %copy-start.4 = (s32[512,1]{0,1:T(1,128)S(1)}, s32[512,1]{0,1:T(1,128)}, u32[]{:S(2)}) copy-start(s32[512,1]{0,1:T(1,128)} %param.8) | copy-start | bytes 6148
  19.4 15.2 %copy-start.5 = (s32[512]{0:T(512)S(1)}, s32[512]{0:T(512)}, u32[]{:S(2)}) copy-start(s32[512]{0:T(512)} %lengths_ref.7) | copy-start | bytes 6148
  19.4 15.2 %collective-permute-start.4 = (bf16[1024,128]{1,0:T(8,128)(2,1)S(1)}, bf16[1024,128]{1,0:T(8,128)(2,1)S(1)}, u32[]{:S(2)}, u32[]{:S(2)}) collective-permute-start(bf16[1024,128]{1,0:T(8,128)(2,1)S(1)} %get-tuple-element.66), channel_id=1, source_target_pairs={{0,4},{1,5},{2,6},{3,7},{4,0},{5,1},{6,2},{7,3},{8,12},{9,13},{10,... | collective-permute-start | bytes 786440 | tf_op jit(solution)/shard_map/ppermute | solution.py:298
  25.8 18.9 %collective-permute-start.5 = (bf16[1024,128]{1,0:T(8,128)(2,1)S(1)}, bf16[1024,128]{1,0:T(8,128)(2,1)S(1)}, u32[]{:S(2)}, u32[]{:S(2)}) collective-permute-start(bf16[1024,128]{1,0:T(8,128)(2,1)S(1)} %get-tuple-element.72), channel_id=1, source_target_pairs={{0,2},{1,3},{2,4},{3,5},{4,6},{5,7},{6,0},{7,1},{8,10},{9,11},{10,... | collective-permute-start | bytes 786440 | tf_op jit(solution)/shard_map/ppermute | solution.py:298
  26.9 21.2 %collective-permute-start.6 = (bf16[1024,128]{1,0:T(8,128)(2,1)S(1)}, bf16[1024,128]{1,0:T(8,128)(2,1)}, u32[]{:S(2)}, u32[]{:S(2)}) collective-permute-start(bf16[1024,128]{1,0:T(8,128)(2,1)S(1)} %get-tuple-element.74), channel_id=1, source_target_pairs={{0,6},{1,7},{2,0},{3,1},{4,2},{5,3},{6,4},{7,5},{8,14},{9,15},{10,... | collective-permute-start | bytes 786440 | tf_op jit(solution)/shard_map/ppermute | solution.py:298
  29.0 19.1 %collective-permute-start.7 = (bf16[1024,128]{1,0:T(8,128)(2,1)S(1)}, bf16[1024,128]{1,0:T(8,128)(2,1)}, u32[]{:S(2)}, u32[]{:S(2)}) collective-permute-start(bf16[1024,128]{1,0:T(8,128)(2,1)S(1)} %get-tuple-element.75), channel_id=1, source_target_pairs={{0,4},{1,5},{2,6},{3,7},{4,0},{5,1},{6,2},{7,3},{8,12},{9,13},{10,... | collective-permute-start | bytes 786440 | tf_op jit(solution)/shard_map/ppermute | solution.py:298
  36.4 24.0 %all-to-all-start = ((bf16[32,64,128]{2,1,0:T(8,128)(2,1)}), bf16[32,64,128]{2,1,0:T(8,128)(2,1)S(1)}, u32[]{:S(2)}, u32[]{:S(2)}) async-start(bf16[32,64,128]{2,1,0:T(8,128)(2,1)} %shard_map.81), calls=%async_computation | async-start | bytes 1048576 | tf_op jit(solution)/shard_map/all_to_all | solution.py:321
  44.7 24.6 %collective-permute-start.8 = (bf16[2048,128]{1,0:T(8,128)(2,1)}, bf16[2048,128]{1,0:T(8,128)(2,1)}, u32[]{:S(2)}, u32[]{:S(2)}) collective-permute-start(bf16[2048,128]{1,0:T(8,128)(2,1)} %get-tuple-element.78), channel_id=1, source_target_pairs={{0,2},{1,3},{2,4},{3,5},{4,6},{5,7},{6,0},{7,1},{8,10},{9,11},{10,... | collective-permute-start | bytes 1572872 | tf_op jit(solution)/shard_map/ppermute | solution.py:298
  45.9 23.4 %collective-permute-start.9 = (bf16[2048,128]{1,0:T(8,128)(2,1)S(1)}, bf16[2048,128]{1,0:T(8,128)(2,1)}, u32[]{:S(2)}, u32[]{:S(2)}) collective-permute-start(bf16[2048,128]{1,0:T(8,128)(2,1)S(1)} %get-tuple-element.79), channel_id=1, source_target_pairs={{0,6},{1,7},{2,0},{3,1},{4,2},{5,3},{6,4},{7,5},{8,14},{9,15},{10,... | collective-permute-start | bytes 1572872 | tf_op jit(solution)/shard_map/ppermute | solution.py:298
  48.0 21.3 %collective-permute-start.10 = (bf16[2048,128]{1,0:T(8,128)(2,1)S(1)}, bf16[2048,128]{1,0:T(8,128)(2,1)}, u32[]{:S(2)}, u32[]{:S(2)}) collective-permute-start(bf16[2048,128]{1,0:T(8,128)(2,1)S(1)} %get-tuple-element.80), channel_id=1, source_target_pairs={{0,4},{1,5},{2,6},{3,7},{4,0},{5,1},{6,2},{7,3},{8,12},{9,13},{10,... | collective-permute-start | bytes 1572872 | tf_op jit(solution)/shard_map/ppermute | solution.py:298
  60.3 26.4 %all-to-all-start.1 = ((bf16[32,64,128]{2,1,0:T(8,128)(2,1)}), bf16[32,64,128]{2,1,0:T(8,128)(2,1)S(1)}, u32[]{:S(2)}, u32[]{:S(2)}) async-start(bf16[32,64,128]{2,1,0:T(8,128)(2,1)} %shard_map.82), calls=%async_computation.1 | async-start | bytes 1048576 | tf_op jit(solution)/shard_map/all_to_all | solution.py:321
  63.9 22.8 %copy-start.2 = (bf16[1,1,16,2,4,1024]{5,4,3,2,1,0:T(4,128)(2,1)S(1)}, bf16[1,1,16,2,4,1024]{5,4,3,2,1,0:T(4,128)(2,1)}, u32[]{:S(2)}) copy-start(bf16[1,1,16,2,4,1024]{5,4,3,2,1,0:T(4,128)(2,1)} %param.10) | copy-start | bytes 786436
  63.9 22.8 %copy-start.3 = (bf16[1,1,16,2,4,256]{5,4,3,2,1,0:T(4,128)(2,1)S(1)}, bf16[1,1,16,2,4,256]{5,4,3,2,1,0:T(4,128)(2,1)}, u32[]{:S(2)}) copy-start(bf16[1,1,16,2,4,256]{5,4,3,2,1,0:T(4,128)(2,1)} %param.11) | copy-start | bytes 196612
  71.4 0.6 copy-start.6
  72.0 23.7 %copy-start.7 = (bf16[2,128,128]{2,1,0:T(8,128)(2,1)S(1)}, bf16[2,128,128]{2,1,0:T(8,128)(2,1)}, u32[]{:S(2)}) copy-start(bf16[2,128,128]{2,1,0:T(8,128)(2,1)} %copy-done.6) | copy-start | bytes 196612
  72.0 18.3 %collective-permute-start.11 = (bf16[2,2,128,128]{3,2,1,0:T(8,128)(2,1)S(1)}, bf16[2,2,128,128]{3,2,1,0:T(8,128)(2,1)S(1)}, u32[]{:S(2)}, u32[]{:S(2)}) collective-permute-start(bf16[2,2,128,128]{3,2,1,0:T(8,128)(2,1)S(1)} %get-tuple-element.81), channel_id=1, source_target_pairs={{0,128},{16,144},{32,160},{48,176},{64,192},{80,208},{96,224},{112... | collective-permute-start | bytes 393224 | tf_op jit(solution)/shard_map/ppermute | solution.py:332
  77.6 17.2 %collective-permute-start.15 = (bf16[2,2,128,128]{3,2,1,0:T(8,128)(2,1)S(1)}, bf16[2,2,128,128]{3,2,1,0:T(8,128)(2,1)S(1)}, u32[]{:S(2)}, u32[]{:S(2)}) collective-permute-start(bf16[2,2,128,128]{3,2,1,0:T(8,128)(2,1)S(1)} %get-tuple-element.89), channel_id=1, source_target_pairs={{0,96},{16,112},{32,128},{48,144},{64,160},{80,176},{96,192},{112,... | collective-permute-start | bytes 393224 | tf_op jit(solution)/shard_map/ppermute | solution.py:332
  78.6 16.2 %collective-permute-start.16 = (bf16[2,2,128,128]{3,2,1,0:T(8,128)(2,1)S(1)}, bf16[2,2,128,128]{3,2,1,0:T(8,128)(2,1)S(1)}, u32[]{:S(2)}, u32[]{:S(2)}) collective-permute-start(bf16[2,2,128,128]{3,2,1,0:T(8,128)(2,1)S(1)} %get-tuple-element.91), channel_id=1, source_target_pairs={{0,160},{16,176},{32,192},{48,208},{64,224},{80,240},{96,0},{112,1... | collective-permute-start | bytes 393224 | tf_op jit(solution)/shard_map/ppermute | solution.py:332
  82.6 16.1 %collective-permute-start.14 = (bf16[2,2,128,128]{3,2,1,0:T(8,128)(2,1)S(1)}, bf16[2,2,128,128]{3,2,1,0:T(8,128)(2,1)S(1)}, u32[]{:S(2)}, u32[]{:S(2)}) collective-permute-start(bf16[2,2,128,128]{3,2,1,0:T(8,128)(2,1)S(1)} %get-tuple-element.88), channel_id=1, source_target_pairs={{0,64},{16,80},{32,96},{48,112},{64,128},{80,144},{96,160},{112,17... | collective-permute-start | bytes 393224 | tf_op jit(solution)/shard_map/ppermute | solution.py:332
  83.2 15.5 %collective-permute-start.17 = (bf16[2,2,128,128]{3,2,1,0:T(8,128)(2,1)S(1)}, bf16[2,2,128,128]{3,2,1,0:T(8,128)(2,1)S(1)}, u32[]{:S(2)}, u32[]{:S(2)}) collective-permute-start(bf16[2,2,128,128]{3,2,1,0:T(8,128)(2,1)S(1)} %get-tuple-element.92), channel_id=1, source_target_pairs={{0,192},{16,208},{32,224},{48,240},{64,0},{80,16},{96,32},{112,48}... | collective-permute-start | bytes 393224 | tf_op jit(solution)/shard_map/ppermute | solution.py:332
  94.8 13.9 %collective-permute-start.20 = (bf16[4,2,128,128]{3,2,1,0:T(8,128)(2,1)S(1)}, bf16[4,2,128,128]{3,2,1,0:T(8,128)(2,1)S(1)}, u32[]{:S(2)}, u32[]{:S(2)}) collective-permute-start(bf16[4,2,128,128]{3,2,1,0:T(8,128)(2,1)S(1)} %shard_map.85), channel_id=1, source_target_pairs={{0,16},{16,0},{32,48},{48,32},{64,80},{80,64},{96,112},{112,96},{1... | collective-permute-start | bytes 786440 | tf_op jit(solution)/shard_map/ppermute | solution.py:369
  95.7 7.8 %collective-permute-start.12 = (bf16[2,128,128]{2,1,0:T(8,128)(2,1)S(1)}, bf16[2,128,128]{2,1,0:T(8,128)(2,1)S(1)}, u32[]{:S(2)}, u32[]{:S(2)}) collective-permute-start(bf16[2,128,128]{2,1,0:T(8,128)(2,1)S(1)} %copy-done.7), channel_id=1, source_target_pairs={{0,32},{16,48},{32,64},{48,80},{64,96},{80,112},{96,128},{112,144}... | collective-permute-start | bytes 196616 | tf_op jit(solution)/shard_map/ppermute | solution.py:334
  98.7 10.0 %collective-permute-start.21 = (bf16[2,2,128,128]{3,2,1,0:T(8,128)(2,1)S(1)}, bf16[2,2,128,128]{3,2,1,0:T(8,128)(2,1)S(1)}, u32[]{:S(2)}, u32[]{:S(2)}) collective-permute-start(bf16[2,2,128,128]{3,2,1,0:T(8,128)(2,1)S(1)} %shard_map.86), channel_id=1, source_target_pairs={{0,16},{16,0},{32,48},{48,32},{64,80},{80,64},{96,112},{112,96},{1... | collective-permute-start | bytes 393224 | tf_op jit(solution)/shard_map/ppermute | solution.py:369
  98.9 6.5 %collective-permute-start.13 = (bf16[2,128,128]{2,1,0:T(8,128)(2,1)S(1)}, bf16[2,128,128]{2,1,0:T(8,128)(2,1)S(1)}, u32[]{:S(2)}, u32[]{:S(2)}) collective-permute-start(bf16[2,128,128]{2,1,0:T(8,128)(2,1)S(1)} %get-tuple-element.87), channel_id=1, source_target_pairs={{0,48},{16,32},{32,80},{48,64},{64,112},{80,96},{96,144},{112,128}... | collective-permute-start | bytes 196616 | tf_op jit(solution)/shard_map/ppermute | solution.py:334
  100.5 4.9 %collective-permute-start.18 = (bf16[2,128,128]{2,1,0:T(8,128)(2,1)S(1)}, bf16[2,128,128]{2,1,0:T(8,128)(2,1)S(1)}, u32[]{:S(2)}, u32[]{:S(2)}) collective-permute-start(bf16[2,128,128]{2,1,0:T(8,128)(2,1)S(1)} %get-tuple-element.93), channel_id=1, source_target_pairs={{0,224},{16,240},{32,0},{48,16},{64,32},{80,48},{96,64},{112,80},{... | collective-permute-start | bytes 196616 | tf_op jit(solution)/shard_map/ppermute | solution.py:334
  103.5 5.2 %collective-permute-start.19 = (bf16[2,128,128]{2,1,0:T(8,128)(2,1)S(1)}, bf16[2,128,128]{2,1,0:T(8,128)(2,1)S(1)}, u32[]{:S(2)}, u32[]{:S(2)}) collective-permute-start(bf16[2,128,128]{2,1,0:T(8,128)(2,1)S(1)} %get-tuple-element.94), channel_id=1, source_target_pairs={{0,240},{16,224},{32,16},{48,0},{64,48},{80,32},{96,80},{112,64},{... | collective-permute-start | bytes 196616 | tf_op jit(solution)/shard_map/ppermute | solution.py:334
